TPU v7x, 32 devices: a whole 2x2x4 slice. The times are simulated.
32 devices in a mesh: dp: 4 (over y, core), fsdp: 4 (over z), seq: 2 (over x).
Axes of the slice: x: 2, y: 2, z: 4, core: 2. Of those that a mesh axis runs over, the one named last changes fastest.
Arguments:
- queries: bfloat16 [16, 256, 2048], P(('dp', 'fsdp'), 'seq'), may hold values from -30 to 30
- key_rows: bfloat16 [16, 256, 2048], P(('dp', 'fsdp'), 'seq'), may hold values from -12 to 12
- value_rows: bfloat16 [16, 256, 2048], P(('dp', 'fsdp'), 'seq'), may hold values from -6 to 6
- cotangent: bfloat16 [16, 256, 2048], P(('dp', 'fsdp'), 'seq'), may hold values from -6 to 6
- out_weight: bfloat16 [2048, 2048], P('fsdp'), may hold values from -0.125 to 0.125
Outputs:
- query_grad: bfloat16 [16, 256, 2048], P(('dp', 'fsdp'), 'seq')
- key_grad: bfloat16 [16, 256, 2048], P(('dp', 'fsdp'), 'seq')
- value_grad: bfloat16 [16, 256, 2048], P(('dp', 'fsdp'), 'seq')
- weight_grad: float32 [2048, 2048], P('fsdp')
All inputs are finite; a program needn't handle non-finite values.
Results may differ from a plain program's by a relative error of at most 0.014.
Values may be sent and summed in bfloat16 or wider, within the bound.
A program may use at most 128 MiB of HBM per device.

v0:
```python
import functools

import jax
import jax.numpy as jnp
from jax import lax
from jax.experimental import pallas as pl
from jax.experimental.pallas import tpu as pltpu
from jax.sharding import PartitionSpec as P

DH = 128
CHUNKS = 4
X_FIRST = (1, 3)
STORES = 8
F32 = jnp.float32
BF16 = jnp.bfloat16


def head_backward(query_head, key_head, value_head, grad_head, block_rows):
    length = key_head.shape[0]
    score_scale = DH ** (-0.5)
    blocks = length // block_rows

    def visit(carry, block):
        key_acc, value_acc = carry
        begin = block * block_rows
        query_block = lax.dynamic_slice_in_dim(query_head, begin, block_rows, 0)
        grad_block = lax.dynamic_slice_in_dim(grad_head, begin, block_rows, 0)
        scores = (
            jnp.einsum("qd,kd->qk", query_block, key_head, preferred_element_type=jnp.float32)
            * score_scale
        )
        highest = jnp.max(scores, axis=1, keepdims=True)
        expanded = jnp.exp(scores - highest)
        weights = expanded / jnp.sum(expanded, axis=1, keepdims=True)
        weights_half = weights.astype(jnp.bfloat16)
        attended = jnp.einsum(
            "qk,kd->qd", weights_half, value_head, preferred_element_type=jnp.float32
        ).astype(jnp.bfloat16)
        grad_weights = jnp.einsum(
            "qd,kd->qk", grad_block, value_head, preferred_element_type=jnp.float32
        )
        row_delta = jnp.sum(weights * grad_weights, axis=1, keepdims=True)
        grad_scores = (weights * (grad_weights - row_delta)).astype(jnp.bfloat16)
        query_grad = (
            jnp.einsum("qk,kd->qd", grad_scores, key_head, preferred_element_type=jnp.float32)
            * score_scale
        ).astype(jnp.bfloat16)
        key_acc = key_acc + jnp.einsum(
            "qk,qd->kd", grad_scores, query_block, preferred_element_type=jnp.float32
        )
        value_acc = value_acc + jnp.einsum(
            "qk,qd->kd", weights_half, grad_block, preferred_element_type=jnp.float32
        )
        return ((key_acc, value_acc), (attended, query_grad))

    empty = jnp.zeros(key_head.shape, jnp.float32)
    finals, stacked = lax.scan(visit, (empty, empty), jnp.arange(blocks))
    attended = stacked[0].reshape(length, DH)
    query_grad = stacked[1].reshape(length, DH)
    key_grad = (finals[0] * score_scale).astype(jnp.bfloat16)
    value_grad = finals[1].astype(jnp.bfloat16)
    return (attended, query_grad, key_grad, value_grad)


def attend_heads(query_heads, key_heads, value_heads, grad_heads):
    length = query_heads.shape[1]
    per_device = query_heads.shape[2] // DH
    block_rows = min(512, length)
    gathered = [[], [], [], []]
    for head_index in range(per_device):
        lower = head_index * DH
        upper = lower + DH
        results = head_backward(
            query_heads[0, :, lower:upper],
            key_heads[0, :, lower:upper],
            value_heads[0, :, lower:upper],
            grad_heads[0, :, lower:upper],
            block_rows,
        )
        for position, result in enumerate(results):
            gathered[position].append(result)
    return tuple((jnp.concatenate(group, axis=1)[None] for group in gathered))


def body(queries, key_rows, value_rows, cotangent, out_weight):
    samples = lax.axis_size("dp") * lax.axis_size("fsdp")
    grad_out = jnp.einsum(
        "btd,rd->btr",
        cotangent,
        lax.all_gather(out_weight, "fsdp", axis=0, tiled=True),
        preferred_element_type=jnp.float32,
    ).astype(jnp.bfloat16)
    query_heads, key_heads, value_heads, grad_heads = (
        lax.all_to_all(queries, "seq", split_axis=2, concat_axis=1, tiled=True),
        lax.all_to_all(key_rows, "seq", split_axis=2, concat_axis=1, tiled=True),
        lax.all_to_all(value_rows, "seq", split_axis=2, concat_axis=1, tiled=True),
        lax.all_to_all(grad_out, "seq", split_axis=2, concat_axis=1, tiled=True),
    )
    head_results = attend_heads(query_heads, key_heads, value_heads, grad_heads)
    attended, query_grad, key_grad, value_grad = (
        lax.all_to_all(head_results[0], "seq", split_axis=1, concat_axis=2, tiled=True),
        lax.all_to_all(head_results[1], "seq", split_axis=1, concat_axis=2, tiled=True),
        lax.all_to_all(head_results[2], "seq", split_axis=1, concat_axis=2, tiled=True),
        lax.all_to_all(head_results[3], "seq", split_axis=1, concat_axis=2, tiled=True),
    )
    shares = lax.psum_scatter(
        jnp.einsum("btr,btd->rd", attended, cotangent, preferred_element_type=jnp.float32),
        ("fsdp", "seq"),
        scatter_dimension=0,
        tiled=True,
    )
    shares = lax.psum(shares.astype(jnp.bfloat16), "dp").astype(jnp.float32)
    total = lax.all_gather(shares.astype(jnp.bfloat16), "seq", axis=0, tiled=True).astype(
        shares.dtype
    )
    return (query_grad, key_grad, value_grad, total / samples)


def dot_nn(a, b):
    return lax.dot_general(a, b, (((1,), (0,)), ((), ())), preferred_element_type=F32)


def dot_nt(a, b):
    return lax.dot_general(a, b, (((1,), (1,)), ((), ())), preferred_element_type=F32)


def dot_tn(a, b):
    return lax.dot_general(a, b, (((0,), (0,)), ((), ())), preferred_element_type=F32)


def fused_kernel(
    nf,
    q_hbm,
    k_hbm,
    v_hbm,
    c_hbm,
    w_hbm,
    qg_hbm,
    kg_hbm,
    vg_hbm,
    wg_hbm,
    cot,
    keys,
    vals,
    go_out,
    go_in,
    at_out,
    at_in,
    probs,
    kv_out,
    kv_in,
    kv_own,
    acc,
    core_out,
    core_in,
    y_out,
    y_in,
    x_out,
    x_in,
    final,
    q_ref,
    w_ref,
    qg_ref,
    kg_ref,
    vg_ref,
    load_sem,
    pair_sem,
    store_sem,
    wide_sem,
    cot_send,
    cot_recv,
    pair_send,
    pair_recv,
    go_send,
    go_recv,
    at_send,
    at_recv,
    kv_send,
    kv_recv,
    rs_send,
    rs_recv,
    ag_send,
    ag_recv,
):
    tokens, width = c_hbm.shape
    rows = w_ref.shape[0]
    group_heads = rows // DH
    scale = DH ** (-0.5)
    dp = lax.axis_index("dp")
    f = lax.axis_index("fsdp")
    s = lax.axis_index("seq")
    core = dp % 2
    half = dp // 2
    sibling = {"dp": half * 2 + (1 - core)}
    across = {"dp": (1 - half) * 2 + core}
    partner = {"seq": 1 - s}

    def remote(src, dst, send, recv, device):
        return pltpu.make_async_remote_copy(
            src_ref=src,
            dst_ref=dst,
            send_sem=send,
            recv_sem=recv,
            device_id=device,
            device_id_type=pl.DeviceIdType.MESH,
        )

    loads = [
        pltpu.make_async_copy(src, dst, load_sem.at[i])
        for i, (src, dst) in enumerate(
            (
                (c_hbm, cot.at[f]),
                (w_hbm, w_ref),
                (q_hbm, q_ref),
            )
        )
    ]

    def group_at(i):
        return (f + 1 + i) % nf

    def pair_load(which, i):
        g = group_at(i)
        cols = pl.ds(pl.multiple_of(g * rows, rows), rows)
        src, dst = ((k_hbm, keys), (v_hbm, vals))[which]
        return pltpu.make_async_copy(src.at[:, cols], dst.at[0, g], pair_sem.at[which, i])

    loads[0].start()
    for i in range(nf):
        pair_load(0, i).start()
        pair_load(1, i).start()
    loads[1].start()
    loads[2].start()

    barrier = pltpu.get_barrier_semaphore()
    for device in (sibling, across, partner):
        pl.semaphore_signal(
            barrier, inc=1, device_id=device, device_id_type=pl.DeviceIdType.MESH
        )
    for step in range(1, nf):
        pl.semaphore_signal(
            barrier,
            inc=1,
            device_id={"fsdp": (f + step) % nf},
            device_id_type=pl.DeviceIdType.MESH,
        )
    pl.semaphore_wait(barrier, 3 + nf - 1)

    def cot_up(j):
        return remote(cot.at[j], cot.at[j], cot_send.at[0, j], cot_recv.at[j], {"fsdp": f + 1})

    def cot_down(j):
        return remote(cot.at[j], cot.at[j], cot_send.at[1, j], cot_recv.at[j], {"fsdp": f - 1})

    def go_copy(j, peer):
        return remote(go_out.at[j], go_in.at[f], go_send.at[j], go_recv.at[f], {"fsdp": peer})

    def at_copy(j, peer):
        return remote(at_out.at[j], at_in.at[f], at_send.at[j], at_recv.at[f], {"fsdp": peer})

    def kv_copy(which, g):
        return remote(
            kv_out.at[which, g],
            kv_in.at[which, g],
            kv_send.at[which, g],
            kv_recv.at[which, g],
            partner,
        )

    def wait_into(ref, sem):
        pltpu.make_async_copy(ref, ref, sem).wait()

    loads[0].wait()

    @pl.when(f + 1 < nf)
    def _():
        cot_up(f).start()

    @pl.when(f > 0)
    def _():
        cot_down(f).start()

    def pair_copy(which, i):
        g = group_at(i)
        buffer = (keys, vals)[which]
        return remote(
            buffer.at[0, g],
            buffer.at[1, g],
            pair_send.at[which, i],
            pair_recv.at[which, i],
            partner,
        )

    for i in range(nf):
        for which in range(2):
            pair_load(which, i).wait()
            pair_copy(which, i).start()

    def project(j):
        return dot_nt(cot[j], w_ref[...]).astype(BF16)

    loads[1].wait()
    go_in[f] = project(f)

    def visit_peers(first, last, action):
        def step(i, carry):
            d = i // 2
            j = f + d * (1 - 2 * (i % 2))

            @pl.when((j >= 0) & (j < nf))
            def _():
                action(j)

            return carry

        lax.fori_loop(2 * first, 2 * last, step, 0)

    def take_cot(j):
        wait_into(cot.at[j], cot_recv.at[j])

        @pl.when((j < f) & (f + 1 < nf))
        def _():
            cot_up(j).start()

        @pl.when((j > f) & (f > 0))
        def _():
            cot_down(j).start()

        go_out[j] = project(j)
        go_copy(j, j).start()

    def soften(i):
        g = group_at(i)
        base = g * rows
        pair_copy(0, i).wait()
        pair_copy(1, i).wait()
        for t in range(group_heads):
            cols = pl.ds(pl.multiple_of(base + t * DH, DH), DH)
            inner = slice(t * DH, (t + 1) * DH)
            kh = keys[:, g, :, inner].reshape(2 * tokens, DH)
            vh = vals[:, g, :, inner].reshape(2 * tokens, DH)
            scores = dot_nt(q_ref[:, cols], kh) * scale
            highest = jnp.max(scores, axis=1, keepdims=True)
            expanded = jnp.exp(scores - highest)
            weights = expanded / jnp.sum(expanded, axis=1, keepdims=True)
            probs[g * group_heads + t] = weights
            at_out[g, :, t * DH : (t + 1) * DH] = dot_nn(weights.astype(BF16), vh).astype(BF16)

        if i == nf - 1:
            at_in[f] = at_out[f]
        else:
            at_copy(g, g).start()


    def differentiate(g):
        base = g * rows
        for t in range(group_heads):
            cols = pl.ds(pl.multiple_of(base + t * DH, DH), DH)
            inner = slice(t * DH, (t + 1) * DH)
            kh = keys[:, g, :, inner].reshape(2 * tokens, DH)
            vh = vals[:, g, :, inner].reshape(2 * tokens, DH)
            qh = q_ref[:, cols]
            gh = go_in[g, :, inner]
            weights = probs[g * group_heads + t]
            grad_weights = dot_nt(gh, vh)
            delta = jnp.sum(weights * grad_weights, axis=1, keepdims=True)
            grad_scores = (weights * (grad_weights - delta)).astype(BF16)
            qg_ref[:, cols] = (dot_nn(grad_scores, kh) * scale).astype(BF16)
            kg = dot_tn(grad_scores, qh) * scale
            vg = dot_tn(weights.astype(BF16), gh)
            kv_own[0, g, :, inner] = kg[:tokens]
            kv_own[1, g, :, inner] = vg[:tokens]
            kv_out[0, g, :, inner] = kg[tokens:].astype(BF16)
            kv_out[1, g, :, inner] = vg[tokens:].astype(BF16)
        kv_copy(0, g).start()
        kv_copy(1, g).start()

    def take_go(j):
        wait_into(go_in.at[j], go_recv.at[j])
        differentiate(j)

    loads[2].wait()
    visit_peers(1, nf - 1, take_cot)
    for d in range(nf):
        soften(d)
    differentiate(f)
    visit_peers(nf - 1, nf, take_cot)
    visit_peers(1, nf - 1, take_go)

    visit_peers(1, nf, lambda j: wait_into(at_in.at[j], at_recv.at[j]))

    part = width // CHUNKS
    core_rows, mid_rows, low_rows = rows // 2, rows // 4, rows // 8

    def bases(c):
        first, second = (s, half) if c in X_FIRST else (half, s)
        mid = core * core_rows + first * mid_rows
        mid_other = core * core_rows + (1 - first) * mid_rows
        low = mid + second * low_rows
        low_other = mid + (1 - second) * low_rows
        return mid, mid_other, low, low_other

    def span(base, count):
        return pl.ds(pl.multiple_of(base, count), count)

    def device_of(stage, c):
        if stage == 0:
            return sibling
        return partner if (stage == 1) == (c in X_FIRST) else across

    def reduce_copy(stage, c):
        src, dst = ((core_out, core_in), (y_out, y_in), (x_out, x_in))[stage]
        device = device_of(stage, c)
        return remote(src.at[c], dst.at[c], rs_send.at[stage, c], rs_recv.at[stage, c], device)

    def gather_copy(stage, c):
        base, count = (
            (core * core_rows, core_rows),
            (bases(c)[0], mid_rows),
            (bases(c)[2], low_rows),
        )[stage]
        block = final.at[c, span(base, count)]
        device = device_of(stage, c)
        return remote(block, block, ag_send.at[stage, c], ag_recv.at[stage, c], device)

    at_all = at_in[...].reshape(nf * tokens, rows)

    for c in range(CHUNKS):
        acc[c] = dot_tn(at_all, cot[:, :, c * part : (c + 1) * part].reshape(nf * tokens, part))
        core_out[c] = acc[c, span((1 - core) * core_rows, core_rows)].astype(BF16)
        reduce_copy(0, c).start()

    def reduce_core(c):
        mid, mid_other, low, low_other = bases(c)
        reduce_copy(0, c).wait_recv()
        there = mid_other - core * core_rows
        y_out[c] = (
            acc[c, span(mid_other, mid_rows)] + core_in[c, span(there, mid_rows)].astype(F32)
        ).astype(BF16)
        reduce_copy(1, c).start()
        here = mid - core * core_rows
        acc[c, span(mid, mid_rows)] += core_in[c, span(here, mid_rows)].astype(F32)

    def reduce_y(c):
        mid, mid_other, low, low_other = bases(c)
        reduce_copy(1, c).wait_recv()
        acc[c, span(mid, mid_rows)] += y_in[c].astype(F32)
        x_out[c] = acc[c, span(low_other, low_rows)].astype(BF16)
        reduce_copy(2, c).start()

    def reduce_x(c):
        low = bases(c)[2]
        reduce_copy(2, c).wait_recv()
        mine = span(low, low_rows)
        final[c, mine] = (acc[c, mine] + x_in[c].astype(F32)).astype(BF16)
        gather_copy(2, c).start()

    def gather_x(c):
        gather_copy(2, c).wait()
        gather_copy(1, c).start()

    def gather_y(c):
        gather_copy(1, c).wait()
        gather_copy(0, c).start()

    def wide_copy(c):
        cols = slice(c * part, (c + 1) * part)
        return pltpu.make_async_copy(final.at[c], wg_hbm.at[:, cols], wide_sem.at[c])

    def gather_core(c):
        gather_copy(0, c).wait()
        wide_copy(c).start()

    def finish(g):
        cols = pl.ds(pl.multiple_of(g * rows, rows), rows)
        for which, out in ((0, kg_ref), (1, vg_ref)):
            kv_copy(which, g).wait()
            out[:, cols] = (kv_own[which, g] + kv_in[which, g].astype(F32)).astype(BF16)

    stores = [
        pltpu.make_async_copy(src, dst, store_sem.at[i])
        for i, (src, dst) in enumerate(((qg_ref, qg_hbm), (kg_ref, kg_hbm), (vg_ref, vg_hbm)))
    ]

    def finish_all():
        finish(f)
        visit_peers(1, nf, finish)
        for store in stores:
            store.start()

    for c in range(CHUNKS):
        reduce_core(c)

    visit_peers(nf - 1, nf, take_go)

    for stage in (reduce_y, reduce_x, gather_x, gather_y):
        for c in range(CHUNKS):
            stage(c)

    finish_all()

    for c in range(CHUNKS):
        gather_core(c)

    for c in range(CHUNKS):
        wide_copy(c).wait()
        for stage in range(3):
            reduce_copy(stage, c).wait_send()

    for store in stores:
        store.wait()

    def drain(j):
        go_copy(j, j).wait_send()
        at_copy(j, j).wait_send()

        @pl.when((j < f) & (f + 1 < nf))
        def _():
            cot_up(j).wait_send()

        @pl.when((j > f) & (f > 0))
        def _():
            cot_down(j).wait_send()

    visit_peers(1, nf, drain)

    @pl.when(f + 1 < nf)
    def _():
        cot_up(f).wait_send()

    @pl.when(f > 0)
    def _():
        cot_down(f).wait_send()


def store_kernel(
    factor,
    qg,
    kg,
    vg,
    wg,
    qg_out,
    kg_out,
    vg_out,
    wg_out,
    held,
    narrow,
    wide,
    sems,
    in_sems,
    out_sems,
):
    count = wg.shape[0] // STORES
    blocks = [slice(i * count, (i + 1) * count) for i in range(STORES)]
    loads = [
        pltpu.make_async_copy(wg.at[block], narrow.at[block], in_sems.at[i])
        for i, block in enumerate(blocks)
    ]
    fills = [
        pltpu.make_async_copy(src, held.at[i], sems.at[0, i]) for i, src in enumerate((qg, kg, vg))
    ]
    copies = [
        pltpu.make_async_copy(held.at[i], dst, sems.at[1, i])
        for i, dst in enumerate((qg_out, kg_out, vg_out))
    ]
    for copy in loads + fills:
        copy.start()
    for i, block in enumerate(blocks):
        loads[i].wait()
        wide[block, :] = narrow[block, :].astype(F32) * factor
        pltpu.make_async_copy(wide.at[block], wg_out.at[block], out_sems.at[i]).start()
    for fill, copy in zip(fills, copies):
        fill.wait()
        copy.start()
    for i, block in enumerate(blocks):
        pltpu.make_async_copy(wide.at[block], wg_out.at[block], out_sems.at[i]).wait()
    for copy in copies:
        copy.wait()


def fused_body(nf, queries, key_rows, value_rows, cotangent, out_weight):
    samples = lax.axis_size("dp") * nf
    tokens, heads_width = queries.shape[1:]
    rows, width = out_weight.shape
    part = width // CHUNKS
    dma = pltpu.SemaphoreType.DMA
    outs = pl.pallas_call(
        functools.partial(fused_kernel, nf),
        out_shape=(
            jax.ShapeDtypeStruct((tokens, heads_width), BF16),
            jax.ShapeDtypeStruct((tokens, heads_width), BF16),
            jax.ShapeDtypeStruct((tokens, heads_width), BF16),
            jax.ShapeDtypeStruct((rows, width), BF16),
        ),
        in_specs=[pl.BlockSpec(memory_space=pltpu.HBM)] * 5,
        out_specs=[pl.BlockSpec(memory_space=pltpu.HBM)] * 4,
        scratch_shapes=[
            pltpu.VMEM((nf, tokens, width), BF16),
            pltpu.VMEM((2, nf, tokens, rows), BF16),
            pltpu.VMEM((2, nf, tokens, rows), BF16),
            pltpu.VMEM((nf, tokens, rows), BF16),
            pltpu.VMEM((nf, tokens, rows), BF16),
            pltpu.VMEM((nf, tokens, rows), BF16),
            pltpu.VMEM((nf, tokens, rows), BF16),
            pltpu.VMEM((heads_width // DH, tokens, 2 * tokens), F32),
            pltpu.VMEM((2, nf, tokens, rows), BF16),
            pltpu.VMEM((2, nf, tokens, rows), BF16),
            pltpu.VMEM((2, nf, tokens, rows), F32),
            pltpu.VMEM((CHUNKS, rows, part), F32),
            pltpu.VMEM((CHUNKS, rows // 2, part), BF16),
            pltpu.VMEM((CHUNKS, rows // 2, part), BF16),
            pltpu.VMEM((CHUNKS, rows // 4, part), BF16),
            pltpu.VMEM((CHUNKS, rows // 4, part), BF16),
            pltpu.VMEM((CHUNKS, rows // 8, part), BF16),
            pltpu.VMEM((CHUNKS, rows // 8, part), BF16),
            pltpu.VMEM((CHUNKS, rows, part), BF16),
            pltpu.VMEM((tokens, heads_width), BF16),
            pltpu.VMEM((rows, width), BF16),
            pltpu.VMEM((tokens, heads_width), BF16),
            pltpu.VMEM((tokens, heads_width), BF16),
            pltpu.VMEM((tokens, heads_width), BF16),
            dma((3,)),
            dma((2, nf)),
            dma((3,)),
            dma((CHUNKS,)),
            dma((2, nf)),
            dma((nf,)),
            dma((2, nf)),
            dma((2, nf)),
            dma((nf,)),
            dma((nf,)),
            dma((nf,)),
            dma((nf,)),
            dma((2, nf)),
            dma((2, nf)),
            dma((3, CHUNKS)),
            dma((3, CHUNKS)),
            dma((3, CHUNKS)),
            dma((3, CHUNKS)),
        ],
        compiler_params=pltpu.CompilerParams(
            collective_id=0, has_side_effects=True, vmem_limit_bytes=58 * 1024 * 1024
        ),
    )(queries[0], key_rows[0], value_rows[0], cotangent[0], out_weight)
    stored = pl.pallas_call(
        functools.partial(store_kernel, 1.0 / samples),
        out_shape=tuple(jax.ShapeDtypeStruct(out.shape, out.dtype) for out in outs[:3])
        + (jax.ShapeDtypeStruct((rows, width), F32),),
        in_specs=[pl.BlockSpec(memory_space=pltpu.HBM)] * 4,
        out_specs=[pl.BlockSpec(memory_space=pltpu.HBM)] * 4,
        scratch_shapes=[
            pltpu.VMEM((3, tokens, heads_width), BF16),
            pltpu.VMEM((rows, width), BF16),
            pltpu.VMEM((rows, width), F32),
            dma((2, 3)),
            dma((STORES,)),
            dma((STORES,)),
        ],
        compiler_params=pltpu.CompilerParams(vmem_limit_bytes=58 * 1024 * 1024),
    )(*outs)
    return tuple(out[None] for out in stored[:3]) + (stored[3],)


def pick_body(mesh):
    if mesh.shape["seq"] == 2 and mesh.shape["dp"] == 4:
        return functools.partial(fused_body, mesh.shape["fsdp"])
    return body


def solution(mesh):
    return jax.shard_map(
        pick_body(mesh),
        mesh=mesh,
        in_specs=(
            P(("dp", "fsdp"), "seq", None),
            P(("dp", "fsdp"), "seq", None),
            P(("dp", "fsdp"), "seq", None),
            P(("dp", "fsdp"), "seq", None),
            P("fsdp", None),
        ),
        out_specs=(
            P(("dp", "fsdp"), "seq", None),
            P(("dp", "fsdp"), "seq", None),
            P(("dp", "fsdp"), "seq", None),
            P("fsdp", None),
        ),
        check_vma=False,
    )
```

profile of v0, /device:TPU:1, one launch (start us, length us, event | category | flops | bytes accessed | tf_op | source)
XLA Modules:
  0.0 96.5 jit_solution(2434132157059402693)
XLA Ops:
  0.6 92.2 %shard_map.84 = (bf16[128,2048]{1,0:T(8,128)(2,1)}, bf16[128,2048]{1,0:T(8,128)(2,1)}, bf16[128,2048]{1,0:T(8,128)(2,1)}, bf16[512,2048]{1,0:T(8,128)(2,1)}) custom-call(bf16[128,2048]{1,0:T(8,128)(2,1)} %bitcast.7, bf16[128,2048]{1,0:T(8,128)(2,1)} %bitcast.8, bf16[128,2048]{1,0:T(8,128)(2,1)} %bitcast.9, bf16[128,2048]{1,0:T(8,128)(2,1)} %bitcast.10, ...), custom_call_target="tpu_custom_call" | custom-call | tf_op jit(solution)/shard_map/pallas_call | solution.py:587
  92.8 3.7 %shard_map.85 = (bf16[128,2048]{1,0:T(8,128)(2,1)}, bf16[128,2048]{1,0:T(8,128)(2,1)}, bf16[128,2048]{1,0:T(8,128)(2,1)}, f32[512,2048]{1,0:T(8,128)}) custom-call(bf16[128,2048]{1,0:T(8,128)(2,1)} %get-tuple-element.12.qg, bf16[128,2048]{1,0:T(8,128)(2,1)} %get-tuple-element.13.kg, bf16[128,2048]{1,0:T(8,128)(2,1)} %get-tuple-element.14.vg, ...), custom_call_target="tpu_custom_call" | custom-call | tf_op jit(solution)/shard_map/pallas_call | solution.py:645
where the time goes:
time: 96.8 us; the launch traced here: 96.5 us
  Pallas kernels  95.9 us (99%)
    pallas_call x1, Pallas kernels, fused_body(): pl.pallas_call(functools.partial(fused_kernel, nf), out_shape=(jax.ShapeD...  92.2 us
    pallas_call x1, Pallas kernels, fused_body(): pl.pallas_call(functools.partial(store_kernel, 1.0 / samples), out_shape=...  3.67 us

commit v1 on v0

v1 whole, which is shorter than its diff:
```python
import functools

import jax
import jax.numpy as jnp
from jax import lax
from jax.experimental import pallas as pl
from jax.experimental.pallas import tpu as pltpu
from jax.sharding import PartitionSpec as P

DH = 128
LOG2E = 1.4426950408889634
CHUNKS = 4
STORES = 8
F32 = jnp.float32
BF16 = jnp.bfloat16


def head_backward(query_head, key_head, value_head, grad_head, block_rows):
    length = key_head.shape[0]
    score_scale = DH ** (-0.5)
    blocks = length // block_rows

    def visit(carry, block):
        key_acc, value_acc = carry
        begin = block * block_rows
        query_block = lax.dynamic_slice_in_dim(query_head, begin, block_rows, 0)
        grad_block = lax.dynamic_slice_in_dim(grad_head, begin, block_rows, 0)
        scores = (
            jnp.einsum("qd,kd->qk", query_block, key_head, preferred_element_type=jnp.float32)
            * score_scale
        )
        highest = jnp.max(scores, axis=1, keepdims=True)
        expanded = jnp.exp(scores - highest)
        weights = expanded / jnp.sum(expanded, axis=1, keepdims=True)
        weights_half = weights.astype(jnp.bfloat16)
        attended = jnp.einsum(
            "qk,kd->qd", weights_half, value_head, preferred_element_type=jnp.float32
        ).astype(jnp.bfloat16)
        grad_weights = jnp.einsum(
            "qd,kd->qk", grad_block, value_head, preferred_element_type=jnp.float32
        )
        row_delta = jnp.sum(weights * grad_weights, axis=1, keepdims=True)
        grad_scores = (weights * (grad_weights - row_delta)).astype(jnp.bfloat16)
        query_grad = (
            jnp.einsum("qk,kd->qd", grad_scores, key_head, preferred_element_type=jnp.float32)
            * score_scale
        ).astype(jnp.bfloat16)
        key_acc = key_acc + jnp.einsum(
            "qk,qd->kd", grad_scores, query_block, preferred_element_type=jnp.float32
        )
        value_acc = value_acc + jnp.einsum(
            "qk,qd->kd", weights_half, grad_block, preferred_element_type=jnp.float32
        )
        return ((key_acc, value_acc), (attended, query_grad))

    empty = jnp.zeros(key_head.shape, jnp.float32)
    finals, stacked = lax.scan(visit, (empty, empty), jnp.arange(blocks))
    attended = stacked[0].reshape(length, DH)
    query_grad = stacked[1].reshape(length, DH)
    key_grad = (finals[0] * score_scale).astype(jnp.bfloat16)
    value_grad = finals[1].astype(jnp.bfloat16)
    return (attended, query_grad, key_grad, value_grad)


def attend_heads(query_heads, key_heads, value_heads, grad_heads):
    length = query_heads.shape[1]
    per_device = query_heads.shape[2] // DH
    block_rows = min(512, length)
    gathered = [[], [], [], []]
    for head_index in range(per_device):
        lower = head_index * DH
        upper = lower + DH
        results = head_backward(
            query_heads[0, :, lower:upper],
            key_heads[0, :, lower:upper],
            value_heads[0, :, lower:upper],
            grad_heads[0, :, lower:upper],
            block_rows,
        )
        for position, result in enumerate(results):
            gathered[position].append(result)
    return tuple((jnp.concatenate(group, axis=1)[None] for group in gathered))


def body(queries, key_rows, value_rows, cotangent, out_weight):
    samples = lax.axis_size("dp") * lax.axis_size("fsdp")
    grad_out = jnp.einsum(
        "btd,rd->btr",
        cotangent,
        lax.all_gather(out_weight, "fsdp", axis=0, tiled=True),
        preferred_element_type=jnp.float32,
    ).astype(jnp.bfloat16)
    query_heads, key_heads, value_heads, grad_heads = (
        lax.all_to_all(queries, "seq", split_axis=2, concat_axis=1, tiled=True),
        lax.all_to_all(key_rows, "seq", split_axis=2, concat_axis=1, tiled=True),
        lax.all_to_all(value_rows, "seq", split_axis=2, concat_axis=1, tiled=True),
        lax.all_to_all(grad_out, "seq", split_axis=2, concat_axis=1, tiled=True),
    )
    head_results = attend_heads(query_heads, key_heads, value_heads, grad_heads)
    attended, query_grad, key_grad, value_grad = (
        lax.all_to_all(head_results[0], "seq", split_axis=1, concat_axis=2, tiled=True),
        lax.all_to_all(head_results[1], "seq", split_axis=1, concat_axis=2, tiled=True),
        lax.all_to_all(head_results[2], "seq", split_axis=1, concat_axis=2, tiled=True),
        lax.all_to_all(head_results[3], "seq", split_axis=1, concat_axis=2, tiled=True),
    )
    shares = lax.psum_scatter(
        jnp.einsum("btr,btd->rd", attended, cotangent, preferred_element_type=jnp.float32),
        ("fsdp", "seq"),
        scatter_dimension=0,
        tiled=True,
    )
    shares = lax.psum(shares.astype(jnp.bfloat16), "dp").astype(jnp.float32)
    total = lax.all_gather(shares.astype(jnp.bfloat16), "seq", axis=0, tiled=True).astype(
        shares.dtype
    )
    return (query_grad, key_grad, value_grad, total / samples)


def dot_nn(a, b):
    return lax.dot_general(a, b, (((1,), (0,)), ((), ())), preferred_element_type=F32)


def dot_nt(a, b):
    return lax.dot_general(a, b, (((1,), (1,)), ((), ())), preferred_element_type=F32)


def dot_tn(a, b):
    return lax.dot_general(a, b, (((0,), (0,)), ((), ())), preferred_element_type=F32)


def fused_kernel(
    nf,
    q_hbm,
    k_hbm,
    v_hbm,
    c_hbm,
    w_hbm,
    gr_hbm,
    wg_hbm,
    cot,
    qkv,
    go_out,
    go_in,
    at_out,
    at_in,
    probs,
    grads,
    w_ref,
    acc,
    y_out,
    y_in,
    x_out,
    x_in,
    final,
    w_sem,
    in_send,
    in_recv,
    cot_z,
    cot_fw,
    cot_sib,
    cot_x,
    cot_recv,
    go_send,
    go_recv,
    at_send,
    at_recv,
    out_send,
    out_recv,
    rs_send,
    rs_recv,
    ag_send,
    ag_recv,
    wide_sem,
):
    tokens, width = c_hbm.shape
    rows = w_hbm.shape[0]
    part = width // CHUNKS
    core_rows = rows // 2
    half_rows = core_rows // 2
    group_heads = core_rows // DH
    length = 2 * tokens
    scale = DH ** (-0.5)
    dp = lax.axis_index("dp")
    f = lax.axis_index("fsdp")
    s = lax.axis_index("seq")
    core = dp % 2
    half = dp // 2
    twin = half * 2 + (1 - core)
    sibling = {"dp": twin}
    across = {"dp": (1 - half) * 2 + core}
    partner = {"seq": 1 - s}
    diagonal = {"dp": twin, "seq": 1 - s}
    native = core == s
    foreign = core != s
    inner = (f > 0) & (f < nf - 1)
    first = 1 + f % 2
    second = (2 + 3 * f) % 5
    third = 6 - f - first - second
    outer = 3 * (f - 1)

    def remote(src, dst, send, recv, device):
        return pltpu.make_async_remote_copy(
            src_ref=src,
            dst_ref=dst,
            send_sem=send,
            recv_sem=recv,
            device_id=device,
            device_id_type=pl.DeviceIdType.MESH,
        )

    def wait_into(ref, sem):
        pltpu.make_async_copy(ref, ref, sem).wait()

    def head_cols(g, c):
        return pl.ds(pl.multiple_of(g * rows + c * core_rows, core_rows), core_rows)

    def chunk(k):
        return c_hbm.at[:, k * part : (k + 1) * part]

    def group_at(i):
        return (f + 1 + i) % nf

    def near_local(which, g):
        src = (q_hbm, k_hbm, v_hbm)[which]
        return pltpu.make_async_copy(
            src.at[:, head_cols(g, core)], qkv.at[which, g, s], in_recv.at[which, g, s]
        )

    def near_copy(which, g):
        src = (q_hbm, k_hbm, v_hbm)[which]
        return remote(
            src.at[:, head_cols(g, core)],
            qkv.at[which, g, s],
            in_send.at[0, which, g],
            in_recv.at[which, g, s],
            {"seq": core},
        )

    def far_copy(which, g):
        src = (q_hbm, k_hbm, v_hbm)[which]
        return remote(
            src.at[:, head_cols(g, 1 - core)],
            qkv.at[which, g, s],
            in_send.at[1, which, g],
            in_recv.at[which, g, s],
            {"dp": twin, "seq": core},
        )

    def own_local(k):
        return pltpu.make_async_copy(chunk(k), cot.at[f, core, k], cot_recv.at[f, core, k])

    def own_z(lane, k, src):
        return remote(
            src,
            cot.at[f, core, k],
            cot_z.at[lane, k],
            cot_recv.at[f, core, k],
            {"fsdp": (first, second)[lane]},
        )

    def to_sibling(j, k, src):
        return remote(src, cot.at[j, core, k], cot_sib.at[j, k], cot_recv.at[j, core, k], sibling)

    def cross(k):
        return remote(
            chunk(k), cot.at[f, 1 - core, k], cot_x.at[k], cot_recv.at[f, 1 - core, k], diagonal
        )

    def passed(i):
        return (3 - f) + i * (3 - 2 * f)

    def pass_on(i, k):
        j = passed(i)
        block = cot.at[j, core, k]
        return remote(block, block, cot_fw.at[i, k], cot_recv.at[j, core, k], {"fsdp": outer})

    def go_copy(j):
        return remote(go_out.at[j], go_in.at[f], go_send.at[j], go_recv.at[f], {"fsdp": j})

    def at_copy(j):
        return remote(at_out.at[j], at_in.at[f], at_send.at[j], at_recv.at[f], {"fsdp": j})

    def home_local(g):
        return pltpu.make_async_copy(
            grads.at[g, s], gr_hbm.at[:, :, head_cols(g, core)], out_recv.at[g, core]
        )

    def home_copy(g, t):
        return remote(
            grads.at[g, t],
            gr_hbm.at[:, :, head_cols(g, core)],
            out_send.at[g, t],
            out_recv.at[g, core],
            {"dp": half * 2 + s, "seq": t},
        )

    w_load = pltpu.make_async_copy(
        w_hbm.at[pl.ds(pl.multiple_of(core * core_rows, core_rows), core_rows), :], w_ref, w_sem
    )

    @pl.when(native)
    def _():
        for i in range(nf):
            for which in range(3):
                near_local(which, group_at(i)).start()

    barrier = pltpu.get_barrier_semaphore()
    for device in (sibling, across, partner, diagonal):
        pl.semaphore_signal(
            barrier, inc=1, device_id=device, device_id_type=pl.DeviceIdType.MESH
        )
    for step in range(1, nf):
        pl.semaphore_signal(
            barrier,
            inc=1,
            device_id={"fsdp": (f + step) % nf},
            device_id_type=pl.DeviceIdType.MESH,
        )
    pl.semaphore_wait(barrier, 4 + nf - 1)

    @pl.when(native)
    def _():
        for which in range(3):
            far_copy(which, group_at(0)).start()
        for k in range(CHUNKS):
            own_z(0, k, chunk(k)).start()
            own_z(1, k, chunk(k)).start()
        for i in range(1, nf):
            for which in range(3):
                far_copy(which, group_at(i)).start()
        for k in range(CHUNKS):
            own_local(k).start()
            to_sibling(f, k, chunk(k)).start()

    @pl.when(foreign)
    def _():
        for i in range(nf):
            for which in range(3):
                near_copy(which, group_at(i)).start()
                far_copy(which, group_at(i)).start()
        for k in range(CHUNKS):
            cross(k).start()

    w_load.start()

    def head_of(which, g, inner_cols):
        return qkv[which, g, :, :, inner_cols].reshape(length, DH)

    def soften(i):
        g = group_at(i)
        for which in range(3):
            for t in range(2):
                wait_into(qkv.at[which, g, t], in_recv.at[which, g, t])
        for t in range(group_heads):
            cols = slice(t * DH, (t + 1) * DH)
            scores = dot_nt(head_of(0, g, cols), head_of(1, g, cols))
            highest = jnp.max(scores, axis=1, keepdims=True)
            expanded = jnp.exp2((scores - highest) * (scale * LOG2E))
            weights = expanded * (1.0 / jnp.sum(expanded, axis=1, keepdims=True))
            probs[g * group_heads + t] = weights
            at_out[g, :, cols] = dot_nn(weights.astype(BF16), head_of(2, g, cols)).astype(BF16)
        if i == nf - 1:
            at_in[f] = at_out[f]
        else:
            at_copy(g).start()

    def differentiate(g):
        for t in range(group_heads):
            cols = slice(t * DH, (t + 1) * DH)
            qh, kh, vh = (head_of(which, g, cols) for which in range(3))
            gh = go_in[g, :, cols]
            weights = probs[g * group_heads + t]
            grad_weights = dot_nt(gh, vh)
            delta = jnp.sum(weights * grad_weights, axis=1, keepdims=True)
            grad_scores = (weights * (grad_weights - delta)).astype(BF16)
            results = (
                dot_nn(grad_scores, kh) * scale,
                dot_tn(grad_scores, qh) * scale,
                dot_tn(weights.astype(BF16), gh),
            )
            for which, result in enumerate(results):
                grads[g, :, which, :, cols] = result.astype(BF16).reshape(2, tokens, DH)
        home_copy(g, 1 - s).start()

        @pl.when(native)
        def _():
            home_local(g).start()

        @pl.when(foreign)
        def _():
            home_copy(g, s).start()

    def project(j):
        total = None
        for k in range(CHUNKS):
            term = dot_nt(
                cot[j, :, k].reshape(length, part), w_ref[:, k * part : (k + 1) * part]
            )
            total = term if total is None else total + term
        return total.astype(BF16)

    def take(j, k):
        wait_into(cot.at[j, core, k], cot_recv.at[j, core, k])

    def take_other(j, k):
        wait_into(cot.at[j, 1 - core, k], cot_recv.at[j, 1 - core, k])

    def share(j, k):
        take(j, k)
        to_sibling(j, k, cot.at[j, core, k]).start()

    def urgent(k):
        @pl.when(inner)
        def _():
            for i in range(2):
                j = passed(i)
                take(j, k)
                pass_on(i, k).start()
                to_sibling(j, k, cot.at[j, core, k]).start()

    def relaxed(k):
        @pl.when(inner)
        def _():
            share(outer, k)

        @pl.when(jnp.logical_not(inner))
        def _():
            share(first, k)
            share(second, k)
            share(third, k)

    for i in range(nf):
        soften(i)

        @pl.when(native)
        def _():
            urgent(i)

    @pl.when(native)
    def _():
        for k in range(CHUNKS):
            take(f, k)
            relaxed(k)

    @pl.when(foreign)
    def _():
        for k in range(CHUNKS):
            take(f, k)
            own_z(0, k, cot.at[f, core, k]).start()
            own_z(1, k, cot.at[f, core, k]).start()
            to_sibling(f, k, cot.at[f, core, k]).start()

    for k in range(CHUNKS):
        take_other(f, k)
    w_load.wait()
    go_in[f] = project(f)
    differentiate(f)

    def mine():
        return pl.ds(pl.multiple_of(half * half_rows, half_rows), half_rows)

    def theirs():
        return pl.ds(pl.multiple_of((1 - half) * half_rows, half_rows), half_rows)

    def reduce_copy(stage, c):
        src, dst = ((y_out, y_in), (x_out, x_in))[stage]
        device = (across, partner)[stage]
        return remote(src.at[c], dst.at[c], rs_send.at[stage, c], rs_recv.at[stage, c], device)

    def gather_copy(stage, c):
        which = half if stage < 2 else 1 - half
        base = core * core_rows + which * half_rows
        block = final.at[c, pl.ds(pl.multiple_of(base, half_rows), half_rows)]
        device = (across, sibling, sibling)[stage]
        return remote(block, block, ag_send.at[stage, c], ag_recv.at[stage, c], device)

    def wide_copy(c):
        cols = slice(c * part, (c + 1) * part)
        return pltpu.make_async_copy(final.at[c], wg_hbm.at[:, cols], wide_sem.at[c])

    def weight_term(c):
        @pl.when(foreign)
        def _():
            urgent(c)
            relaxed(c)

        for d in (first, second, third):
            take_other(d, c)
        if c == 0:
            for d in (first, second, third):
                wait_into(at_in.at[d], at_recv.at[d])
        at_all = at_in[...].reshape(nf * length, core_rows)
        acc[c] = dot_tn(at_all, cot[:, :, c].reshape(nf * length, part))
        y_out[c] = acc[c, theirs()].astype(BF16)
        reduce_copy(0, c).start()

    def reduce_y(c):
        reduce_copy(0, c).wait_recv()
        x_out[c] = (acc[c, mine()] + y_in[c].astype(F32)).astype(BF16)
        reduce_copy(1, c).start()

    def reduce_x(c):
        reduce_copy(1, c).wait_recv()
        base = core * core_rows + half * half_rows
        final[c, pl.ds(pl.multiple_of(base, half_rows), half_rows)] = (
            x_out[c].astype(F32) + x_in[c].astype(F32)
        ).astype(BF16)
        gather_copy(0, c).start()
        gather_copy(1, c).start()

    def gather_y(c):
        gather_copy(0, c).wait_recv()
        gather_copy(2, c).start()

    def gather_core(c):
        gather_copy(1, c).wait_recv()
        gather_copy(2, c).wait_recv()
        wide_copy(c).start()

    def send_go(j):
        go_out[j] = project(j)
        go_copy(j).start()

    def take_go(j):
        wait_into(go_in.at[j], go_recv.at[j])
        differentiate(j)

    weight_term(0)
    weight_term(1)
    reduce_y(0)
    weight_term(2)
    reduce_y(1)
    reduce_x(0)
    weight_term(3)
    send_go(first)
    send_go(second)
    send_go(third)
    reduce_y(2)
    reduce_x(1)
    gather_y(0)
    reduce_y(3)
    take_go(first)
    reduce_x(2)
    gather_y(1)
    gather_core(0)
    reduce_x(3)
    take_go(second)
    gather_y(2)
    gather_core(1)
    gather_y(3)
    take_go(third)
    gather_core(2)
    gather_core(3)

    for g in range(nf):
        for c in range(2):
            wait_into(gr_hbm.at[:, :, head_cols(g, c)], out_recv.at[g, c])
    for c in range(CHUNKS):
        wide_copy(c).wait()

    for c in range(CHUNKS):
        for stage in range(2):
            reduce_copy(stage, c).wait_send()
        for stage in range(3):
            gather_copy(stage, c).wait_send()
    for j in (first, second, third):
        go_copy(j).wait_send()
        at_copy(j).wait_send()
    for g in range(nf):
        home_copy(g, 1 - s).wait_send()
        for which in range(3):
            far_copy(which, g).wait_send()
    for k in range(CHUNKS):
        own_z(0, k, cot.at[f, core, k]).wait_send()
        own_z(1, k, cot.at[f, core, k]).wait_send()
        for j in range(nf):
            to_sibling(j, k, cot.at[j, core, k]).wait_send()

    @pl.when(inner)
    def _():
        for k in range(CHUNKS):
            for i in range(2):
                pass_on(i, k).wait_send()

    @pl.when(foreign)
    def _():
        for g in range(nf):
            home_copy(g, s).wait_send()
            for which in range(3):
                near_copy(which, g).wait_send()
        for k in range(CHUNKS):
            cross(k).wait_send()


def store_kernel(
    factor,
    gr,
    wg,
    qg_out,
    kg_out,
    vg_out,
    wg_out,
    held,
    narrow,
    wide,
    sems,
    in_sems,
    out_sems,
):
    count = wg.shape[0] // STORES
    blocks = [slice(i * count, (i + 1) * count) for i in range(STORES)]
    loads = [
        pltpu.make_async_copy(wg.at[block], narrow.at[block], in_sems.at[i])
        for i, block in enumerate(blocks)
    ]
    fills = [pltpu.make_async_copy(gr.at[i], held.at[i], sems.at[0, i]) for i in range(3)]
    copies = [
        pltpu.make_async_copy(held.at[i], dst, sems.at[1, i])
        for i, dst in enumerate((qg_out, kg_out, vg_out))
    ]
    for copy in loads + fills:
        copy.start()
    for i, block in enumerate(blocks):
        loads[i].wait()
        wide[block, :] = narrow[block, :].astype(F32) * factor
        pltpu.make_async_copy(wide.at[block], wg_out.at[block], out_sems.at[i]).start()
    for fill, copy in zip(fills, copies):
        fill.wait()
        copy.start()
    for i, block in enumerate(blocks):
        pltpu.make_async_copy(wide.at[block], wg_out.at[block], out_sems.at[i]).wait()
    for copy in copies:
        copy.wait()


def fused_body(nf, queries, key_rows, value_rows, cotangent, out_weight):
    samples = lax.axis_size("dp") * nf
    tokens, heads_width = queries.shape[1:]
    rows, width = out_weight.shape
    part = width // CHUNKS
    core_rows = rows // 2
    half_rows = core_rows // 2
    length = 2 * tokens
    heads = heads_width // DH // 2
    dma = pltpu.SemaphoreType.DMA
    outs = pl.pallas_call(
        functools.partial(fused_kernel, nf),
        out_shape=(
            jax.ShapeDtypeStruct((3, tokens, heads_width), BF16),
            jax.ShapeDtypeStruct((rows, width), BF16),
        ),
        in_specs=[pl.BlockSpec(memory_space=pltpu.HBM)] * 5,
        out_specs=[pl.BlockSpec(memory_space=pltpu.HBM)] * 2,
        scratch_shapes=[
            pltpu.VMEM((nf, 2, CHUNKS, tokens, part), BF16),
            pltpu.VMEM((3, nf, 2, tokens, core_rows), BF16),
            pltpu.VMEM((nf, length, core_rows), BF16),
            pltpu.VMEM((nf, length, core_rows), BF16),
            pltpu.VMEM((nf, length, core_rows), BF16),
            pltpu.VMEM((nf, length, core_rows), BF16),
            pltpu.VMEM((heads, length, length), F32),
            pltpu.VMEM((nf, 2, 3, tokens, core_rows), BF16),
            pltpu.VMEM((core_rows, width), BF16),
            pltpu.VMEM((CHUNKS, core_rows, part), F32),
            pltpu.VMEM((CHUNKS, half_rows, part), BF16),
            pltpu.VMEM((CHUNKS, half_rows, part), BF16),
            pltpu.VMEM((CHUNKS, half_rows, part), BF16),
            pltpu.VMEM((CHUNKS, half_rows, part), BF16),
            pltpu.VMEM((CHUNKS, rows, part), BF16),
            dma,
            dma((2, 3, nf)),
            dma((3, nf, 2)),
            dma((2, CHUNKS)),
            dma((2, CHUNKS)),
            dma((nf, CHUNKS)),
            dma((CHUNKS,)),
            dma((nf, 2, CHUNKS)),
            dma((nf,)),
            dma((nf,)),
            dma((nf,)),
            dma((nf,)),
            dma((nf, 2)),
            dma((nf, 2)),
            dma((2, CHUNKS)),
            dma((2, CHUNKS)),
            dma((3, CHUNKS)),
            dma((3, CHUNKS)),
            dma((CHUNKS,)),
        ],
        compiler_params=pltpu.CompilerParams(
            collective_id=0, has_side_effects=True, vmem_limit_bytes=58 * 1024 * 1024
        ),
    )(queries[0], key_rows[0], value_rows[0], cotangent[0], out_weight)
    stored = pl.pallas_call(
        functools.partial(store_kernel, 1.0 / samples),
        out_shape=(jax.ShapeDtypeStruct((tokens, heads_width), BF16),) * 3
        + (jax.ShapeDtypeStruct((rows, width), F32),),
        in_specs=[pl.BlockSpec(memory_space=pltpu.HBM)] * 2,
        out_specs=[pl.BlockSpec(memory_space=pltpu.HBM)] * 4,
        scratch_shapes=[
            pltpu.VMEM((3, tokens, heads_width), BF16),
            pltpu.VMEM((rows, width), BF16),
            pltpu.VMEM((rows, width), F32),
            dma((2, 3)),
            dma((STORES,)),
            dma((STORES,)),
        ],
        compiler_params=pltpu.CompilerParams(vmem_limit_bytes=58 * 1024 * 1024),
    )(*outs)
    return tuple(out[None] for out in stored[:3]) + (stored[3],)


def pick_body(mesh):
    if mesh.shape["seq"] == 2 and mesh.shape["dp"] == 4 and mesh.shape["fsdp"] == 4:
        return functools.partial(fused_body, mesh.shape["fsdp"])
    return body


def solution(mesh):
    return jax.shard_map(
        pick_body(mesh),
        mesh=mesh,
        in_specs=(
            P(("dp", "fsdp"), "seq", None),
            P(("dp", "fsdp"), "seq", None),
            P(("dp", "fsdp"), "seq", None),
            P(("dp", "fsdp"), "seq", None),
            P("fsdp", None),
        ),
        out_specs=(
            P(("dp", "fsdp"), "seq", None),
            P(("dp", "fsdp"), "seq", None),
            P(("dp", "fsdp"), "seq", None),
            P("fsdp", None),
        ),
        check_vma=False,
    )
```

time: 96.8 us -> 85.3 us (0.88)
  Pallas kernels: 95.9 us -> 84 us
    pallas_call x1, Pallas kernels: 92.2 us -> 80.3 us  [fused_body(): pl.pallas_call(functools.partial(fused_kernel, nf), out_shape=(jax.ShapeD...]
where the time goes in v1:
time: 85.3 us; the launch traced here: 84.6 us
  Pallas kernels  84 us (98%)
    pallas_call x1, Pallas kernels, fused_body(): pl.pallas_call(functools.partial(fused_kernel, nf), out_shape=(jax.ShapeD...  80.3 us
    pallas_call x1, Pallas kernels, fused_body(): pl.pallas_call(functools.partial(store_kernel, 1.0 / samples), out_shape=...  3.67 us

profile of v1, /device:TPU:1, one launch (start us, length us, event | category | flops | bytes accessed | tf_op | source)
XLA Modules:
  0.0 84.6 jit_solution(17039612545581056644)
XLA Ops:
  0.6 80.3 %shard_map.84 = (bf16[3,128,2048]{2,1,0:T(8,128)(2,1)}, bf16[512,2048]{1,0:T(8,128)(2,1)}) custom-call(bf16[128,2048]{1,0:T(8,128)(2,1)} %bitcast.7, bf16[128,2048]{1,0:T(8,128)(2,1)} %bitcast.8, bf16[128,2048]{1,0:T(8,128)(2,1)} %bitcast.9, bf16[128,2048]{1,0:T(8,128)(2,1)} %bitcast.10, bf16[512,2048]{1,0:T(8,128)(2,1)} %w_hbm.1), custom_call_target="tpu_custom_call" | custom-call | tf_op jit(solution)/shard_map/pallas_call | solution.py:646
  80.9 3.7 %shard_map.85 = (bf16[128,2048]{1,0:T(8,128)(2,1)}, bf16[128,2048]{1,0:T(8,128)(2,1)}, bf16[128,2048]{1,0:T(8,128)(2,1)}, f32[512,2048]{1,0:T(8,128)}) custom-call(bf16[3,128,2048]{2,1,0:T(8,128)(2,1)} %get-tuple-element.10.gr, bf16[512,2048]{1,0:T(8,128)(2,1)} %get-tuple-element.11.wg), custom_call_target="tpu_custom_call" | custom-call | tf_op jit(solution)/shard_map/pallas_call | solution.py:694

commit v2 on v1

--- a/solution.py
+++ b/solution.py
@@ -151,6 +151,8 @@
     y_in,
     x_out,
     x_in,
+    d_out,
+    d_in,
     final,
     w_sem,
     in_send,
@@ -170,6 +172,12 @@
     rs_recv,
     ag_send,
     ag_recv,
+    ds_send,
+    ds_recv,
+    dg_send,
+    dg_recv,
+    df_send,
+    df_recv,
     wide_sem,
 ):
     tokens, width = c_hbm.shape
@@ -196,7 +204,9 @@
     first = 1 + f % 2
     second = (2 + 3 * f) % 5
     third = 6 - f - first - second
-    outer = 3 * (f - 1)
+    end = 3 * (f - 1)
+    outer = jnp.logical_not(inner)
+    corner = {"dp": (1 - half) * 2 + core, "seq": 1 - s}
 
     def remote(src, dst, send, recv, device):
         return pltpu.make_async_remote_copy(
@@ -272,7 +282,7 @@
     def pass_on(i, k):
         j = passed(i)
         block = cot.at[j, core, k]
-        return remote(block, block, cot_fw.at[i, k], cot_recv.at[j, core, k], {"fsdp": outer})
+        return remote(block, block, cot_fw.at[i, k], cot_recv.at[j, core, k], {"fsdp": end})
 
     def go_copy(j):
         return remote(go_out.at[j], go_in.at[f], go_send.at[j], go_recv.at[f], {"fsdp": j})
@@ -305,7 +315,7 @@
                 near_local(which, group_at(i)).start()
 
     barrier = pltpu.get_barrier_semaphore()
-    for device in (sibling, across, partner, diagonal):
+    for device in (sibling, across, partner, diagonal, corner):
         pl.semaphore_signal(
             barrier, inc=1, device_id=device, device_id_type=pl.DeviceIdType.MESH
         )
@@ -316,16 +326,14 @@
             device_id={"fsdp": (f + step) % nf},
             device_id_type=pl.DeviceIdType.MESH,
         )
-    pl.semaphore_wait(barrier, 4 + nf - 1)
+    pl.semaphore_wait(barrier, 5 + nf - 1)
 
     @pl.when(native)
     def _():
-        for which in range(3):
-            far_copy(which, group_at(0)).start()
         for k in range(CHUNKS):
             own_z(0, k, chunk(k)).start()
             own_z(1, k, chunk(k)).start()
-        for i in range(1, nf):
+        for i in range(nf):
             for which in range(3):
                 far_copy(which, group_at(i)).start()
         for k in range(CHUNKS):
@@ -338,8 +346,7 @@
             for which in range(3):
                 near_copy(which, group_at(i)).start()
                 far_copy(which, group_at(i)).start()
-        for k in range(CHUNKS):
-            cross(k).start()
+            cross(i).start()
 
     w_load.start()
 
@@ -418,37 +425,47 @@
                 pass_on(i, k).start()
                 to_sibling(j, k, cot.at[j, core, k]).start()
 
-    def relaxed(k):
-        @pl.when(inner)
-        def _():
-            share(outer, k)
-
-        @pl.when(jnp.logical_not(inner))
-        def _():
-            share(first, k)
-            share(second, k)
-            share(third, k)
-
-    for i in range(nf):
-        soften(i)
-
+    def pass_own(k):
+        take(f, k)
+        own_z(0, k, cot.at[f, core, k]).start()
+        own_z(1, k, cot.at[f, core, k]).start()
+        to_sibling(f, k, cot.at[f, core, k]).start()
+
+    def for_native(*chunks):
         @pl.when(native)
         def _():
-            urgent(i)
+            for k in chunks:
+                urgent(k)
+
+    def for_foreign(*chunks):
+        @pl.when(foreign)
+        def _():
+            for k in chunks:
+                urgent(k)
+
+    def for_own(k):
+        @pl.when(foreign)
+        def _():
+            pass_own(k)
+
+    for_native(0)
+    soften(0)
+    for_native(1)
+    for_own(0)
+    soften(1)
+    for_native(2)
+    for_own(1)
+    soften(2)
+    for_native(3)
+    for_own(2)
+    for_foreign(0)
+    soften(3)
+    for_own(3)
 
     @pl.when(native)
     def _():
         for k in range(CHUNKS):
             take(f, k)
-            relaxed(k)
-
-    @pl.when(foreign)
-    def _():
-        for k in range(CHUNKS):
-            take(f, k)
-            own_z(0, k, cot.at[f, core, k]).start()
-            own_z(1, k, cot.at[f, core, k]).start()
-            to_sibling(f, k, cot.at[f, core, k]).start()
 
     for k in range(CHUNKS):
         take_other(f, k)
@@ -478,21 +495,65 @@
         cols = slice(c * part, (c + 1) * part)
         return pltpu.make_async_copy(final.at[c], wg_hbm.at[:, cols], wide_sem.at[c])
 
+    last = CHUNKS - 1
+
+    def quarter_of(h, t):
+        count = half_rows // 2
+        return pl.ds(pl.multiple_of((h * 2 + t) * count, count), count)
+
+    others = ((half, 1 - s, partner), (1 - half, s, across), (1 - half, 1 - s, corner))
+
+    def direct_copy(i):
+        h, t, device = others[i]
+        return remote(d_out.at[quarter_of(h, t)], d_in.at[i], ds_send.at[i], ds_recv.at[i], device)
+
+    def piece(c, h, t):
+        base = core * core_rows + (h * 2 + t) * (half_rows // 2)
+        return final.at[last, pl.ds(pl.multiple_of(base, half_rows // 2), half_rows // 2)]
+
+    def spread_copy(i):
+        block = piece(core, half, s)
+        device = (partner, across, corner, sibling)[i]
+        return remote(block, block, dg_send.at[i], dg_recv.at[i], device)
+
+    def relay_copy(i):
+        h, t, _ = others[i]
+        block = piece(core, h, t)
+        return remote(block, block, df_send.at[i], df_recv.at[i], sibling)
+
     def weight_term(c):
-        @pl.when(foreign)
-        def _():
-            urgent(c)
-            relaxed(c)
-
-        for d in (first, second, third):
-            take_other(d, c)
         if c == 0:
             for d in (first, second, third):
                 wait_into(at_in.at[d], at_recv.at[d])
         at_all = at_in[...].reshape(nf * length, core_rows)
         acc[c] = dot_tn(at_all, cot[:, :, c].reshape(nf * length, part))
-        y_out[c] = acc[c, theirs()].astype(BF16)
-        reduce_copy(0, c).start()
+        if c < last:
+            y_out[c] = acc[c, theirs()].astype(BF16)
+            reduce_copy(0, c).start()
+        else:
+            d_out[...] = acc[c].astype(BF16)
+            for i in (2, 1, 0):
+                direct_copy(i).start()
+
+    def reduce_direct(c):
+        total = acc[last, quarter_of(half, s)]
+        for i in range(3):
+            direct_copy(i).wait_recv()
+            total = total + d_in[i].astype(F32)
+        piece(core, half, s)[...] = total.astype(BF16)
+        for i in (2, 1, 0, 3):
+            spread_copy(i).start()
+
+    def gather_direct(c):
+        for i in range(3):
+            spread_copy(i).wait_recv()
+            relay_copy(i).start()
+
+    def gather_last(c):
+        spread_copy(3).wait_recv()
+        for i in range(3):
+            relay_copy(i).wait_recv()
+        wide_copy(last).start()
 
     def reduce_y(c):
         reduce_copy(0, c).wait_recv()
@@ -525,32 +586,100 @@
         wait_into(go_in.at[j], go_recv.at[j])
         differentiate(j)
 
-    weight_term(0)
-    weight_term(1)
-    reduce_y(0)
-    weight_term(2)
-    reduce_y(1)
-    reduce_x(0)
-    weight_term(3)
-    send_go(first)
-    send_go(second)
-    send_go(third)
-    reduce_y(2)
-    reduce_x(1)
-    gather_y(0)
-    reduce_y(3)
-    take_go(first)
-    reduce_x(2)
-    gather_y(1)
-    gather_core(0)
-    reduce_x(3)
-    take_go(second)
-    gather_y(2)
-    gather_core(1)
-    gather_y(3)
-    take_go(third)
-    gather_core(2)
-    gather_core(3)
+    def arrive(j, k):
+        share(j, k)
+        take_other(j, k)
+
+    def all_arrive(k):
+        for j in (first, second, third):
+            share(j, k)
+        for j in (first, second, third):
+            take_other(j, k)
+
+    def end_arrives(k):
+        arrive(second, k)
+
+    def passed_arrive(k):
+        if k > 0:
+            for_foreign(k)
+        take_other(first, k)
+        take_other(third, k)
+
+    def play(*steps):
+        for action, argument in steps:
+            action(argument)
+
+    @pl.when(inner)
+    def _():
+        play(
+            (end_arrives, 0),
+            (passed_arrive, 0),
+            (weight_term, 0),
+            (end_arrives, 1),
+            (passed_arrive, 1),
+            (weight_term, 1),
+            (end_arrives, 2),
+            (end_arrives, 3),
+            (send_go, second),
+            (reduce_y, 0),
+            (passed_arrive, 2),
+            (weight_term, 2),
+            (reduce_y, 1),
+            (passed_arrive, 3),
+            (weight_term, 3),
+            (send_go, third),
+            (send_go, first),
+            (reduce_x, 0),
+            (reduce_y, 2),
+            (take_go, first),
+            (reduce_x, 1),
+            (gather_y, 0),
+            (reduce_direct, last),
+            (reduce_x, 2),
+            (gather_y, 1),
+            (gather_core, 0),
+            (take_go, third),
+            (gather_direct, last),
+            (take_go, second),
+            (gather_y, 2),
+            (gather_core, 1),
+            (gather_last, last),
+            (gather_core, 2),
+        )
+
+    @pl.when(outer)
+    def _():
+        play(
+            (all_arrive, 0),
+            (weight_term, 0),
+            (all_arrive, 1),
+            (weight_term, 1),
+            (reduce_y, 0),
+            (take_go, first),
+            (all_arrive, 2),
+            (weight_term, 2),
+            (reduce_y, 1),
+            (reduce_x, 0),
+            (all_arrive, 3),
+            (weight_term, 3),
+            (send_go, third),
+            (send_go, second),
+            (send_go, first),
+            (reduce_y, 2),
+            (reduce_x, 1),
+            (gather_y, 0),
+            (take_go, second),
+            (reduce_direct, last),
+            (gather_y, 1),
+            (gather_core, 0),
+            (take_go, third),
+            (reduce_x, 2),
+            (gather_direct, last),
+            (gather_core, 1),
+            (gather_y, 2),
+            (gather_last, last),
+            (gather_core, 2),
+        )
 
     for g in range(nf):
         for c in range(2):
@@ -559,10 +688,17 @@
         wide_copy(c).wait()
 
     for c in range(CHUNKS):
+        if c == last:
+            continue
         for stage in range(2):
             reduce_copy(stage, c).wait_send()
         for stage in range(3):
             gather_copy(stage, c).wait_send()
+    for i in range(3):
+        direct_copy(i).wait_send()
+        relay_copy(i).wait_send()
+    for i in range(4):
+        spread_copy(i).wait_send()
     for j in (first, second, third):
         go_copy(j).wait_send()
         at_copy(j).wait_send()
@@ -666,6 +802,8 @@
             pltpu.VMEM((CHUNKS, half_rows, part), BF16),
             pltpu.VMEM((CHUNKS, half_rows, part), BF16),
             pltpu.VMEM((CHUNKS, half_rows, part), BF16),
+            pltpu.VMEM((core_rows, part), BF16),
+            pltpu.VMEM((3, half_rows // 2, part), BF16),
             pltpu.VMEM((CHUNKS, rows, part), BF16),
             dma,
             dma((2, 3, nf)),
@@ -685,6 +823,12 @@
             dma((2, CHUNKS)),
             dma((3, CHUNKS)),
             dma((3, CHUNKS)),
+            dma((3,)),
+            dma((3,)),
+            dma((4,)),
+            dma((4,)),
+            dma((3,)),
+            dma((3,)),
             dma((CHUNKS,)),
         ],
         compiler_params=pltpu.CompilerParams(

time: 85.3 us -> 82.2 us (0.964)
  Pallas kernels: 84 us -> 81.2 us
    pallas_call x1, Pallas kernels: 80.3 us -> 77.6 us  [fused_body(): pl.pallas_call(functools.partial(fused_kernel, nf), out_shape=(jax.ShapeD...]
where the time goes in v2:
time: 82.2 us; the launch traced here: 82 us
  Pallas kernels  81.2 us (99%)
    pallas_call x1, Pallas kernels, fused_body(): pl.pallas_call(functools.partial(fused_kernel, nf), out_shape=(jax.ShapeD...  77.6 us
    pallas_call x1, Pallas kernels, fused_body(): pl.pallas_call(functools.partial(store_kernel, 1.0 / samples), out_shape=...  3.67 us

profile of v2, /device:TPU:1, one launch (start us, length us, event | category | flops | bytes accessed | tf_op | source)
XLA Modules:
  0.0 82.0 jit_solution(5635377961652973838)
XLA Ops:
  0.6 77.6 %shard_map.84 = (bf16[3,128,2048]{2,1,0:T(8,128)(2,1)}, bf16[512,2048]{1,0:T(8,128)(2,1)}) custom-call(bf16[128,2048]{1,0:T(8,128)(2,1)} %bitcast.7, bf16[128,2048]{1,0:T(8,128)(2,1)} %bitcast.8, bf16[128,2048]{1,0:T(8,128)(2,1)} %bitcast.9, bf16[128,2048]{1,0:T(8,128)(2,1)} %bitcast.10, bf16[512,2048]{1,0:T(8,128)(2,1)} %w_hbm.1), custom_call_target="tpu_custom_call" | custom-call | tf_op jit(solution)/shard_map/pallas_call | solution.py:782
  78.2 3.7 %shard_map.85 = (bf16[128,2048]{1,0:T(8,128)(2,1)}, bf16[128,2048]{1,0:T(8,128)(2,1)}, bf16[128,2048]{1,0:T(8,128)(2,1)}, f32[512,2048]{1,0:T(8,128)}) custom-call(bf16[3,128,2048]{2,1,0:T(8,128)(2,1)} %get-tuple-element.10.gr, bf16[512,2048]{1,0:T(8,128)(2,1)} %get-tuple-element.11.wg), custom_call_target="tpu_custom_call" | custom-call | tf_op jit(solution)/shard_map/pallas_call | solution.py:838

commit v3 on v2

--- a/solution.py
+++ b/solution.py
@@ -135,8 +135,8 @@
     v_hbm,
     c_hbm,
     w_hbm,
-    gr_hbm,
-    wg_hbm,
+    gr_ref,
+    final,
     cot,
     qkv,
     go_out,
@@ -153,7 +153,6 @@
     x_in,
     d_out,
     d_in,
-    final,
     w_sem,
     in_send,
     in_recv,
@@ -178,7 +177,6 @@
     dg_recv,
     df_send,
     df_recv,
-    wide_sem,
 ):
     tokens, width = c_hbm.shape
     rows = w_hbm.shape[0]
@@ -292,13 +290,13 @@
 
     def home_local(g):
         return pltpu.make_async_copy(
-            grads.at[g, s], gr_hbm.at[:, :, head_cols(g, core)], out_recv.at[g, core]
+            grads.at[g, s], gr_ref.at[:, :, head_cols(g, core)], out_recv.at[g, core]
         )
 
     def home_copy(g, t):
         return remote(
             grads.at[g, t],
-            gr_hbm.at[:, :, head_cols(g, core)],
+            gr_ref.at[:, :, head_cols(g, core)],
             out_send.at[g, t],
             out_recv.at[g, core],
             {"dp": half * 2 + s, "seq": t},
@@ -491,10 +489,6 @@
         device = (across, sibling, sibling)[stage]
         return remote(block, block, ag_send.at[stage, c], ag_recv.at[stage, c], device)
 
-    def wide_copy(c):
-        cols = slice(c * part, (c + 1) * part)
-        return pltpu.make_async_copy(final.at[c], wg_hbm.at[:, cols], wide_sem.at[c])
-
     last = CHUNKS - 1
 
     def quarter_of(h, t):
@@ -553,7 +547,6 @@
         spread_copy(3).wait_recv()
         for i in range(3):
             relay_copy(i).wait_recv()
-        wide_copy(last).start()
 
     def reduce_y(c):
         reduce_copy(0, c).wait_recv()
@@ -576,7 +569,6 @@
     def gather_core(c):
         gather_copy(1, c).wait_recv()
         gather_copy(2, c).wait_recv()
-        wide_copy(c).start()
 
     def send_go(j):
         go_out[j] = project(j)
@@ -683,10 +675,7 @@
 
     for g in range(nf):
         for c in range(2):
-            wait_into(gr_hbm.at[:, :, head_cols(g, c)], out_recv.at[g, c])
-    for c in range(CHUNKS):
-        wide_copy(c).wait()
-
+            wait_into(gr_ref.at[:, :, head_cols(g, c)], out_recv.at[g, c])
     for c in range(CHUNKS):
         if c == last:
             continue
@@ -728,43 +717,23 @@
             cross(k).wait_send()
 
 
-def store_kernel(
-    factor,
-    gr,
-    wg,
-    qg_out,
-    kg_out,
-    vg_out,
-    wg_out,
-    held,
-    narrow,
-    wide,
-    sems,
-    in_sems,
-    out_sems,
-):
-    count = wg.shape[0] // STORES
-    blocks = [slice(i * count, (i + 1) * count) for i in range(STORES)]
-    loads = [
-        pltpu.make_async_copy(wg.at[block], narrow.at[block], in_sems.at[i])
-        for i, block in enumerate(blocks)
-    ]
-    fills = [pltpu.make_async_copy(gr.at[i], held.at[i], sems.at[0, i]) for i in range(3)]
+def store_kernel(factor, gr, wg, qg_out, kg_out, vg_out, wg_out, wide, sems, out_sems):
+    count = wg.shape[1] // STORES
+    part = wg.shape[2]
     copies = [
-        pltpu.make_async_copy(held.at[i], dst, sems.at[1, i])
+        pltpu.make_async_copy(gr.at[i], dst, sems.at[i])
         for i, dst in enumerate((qg_out, kg_out, vg_out))
     ]
-    for copy in loads + fills:
-        copy.start()
-    for i, block in enumerate(blocks):
-        loads[i].wait()
-        wide[block, :] = narrow[block, :].astype(F32) * factor
-        pltpu.make_async_copy(wide.at[block], wg_out.at[block], out_sems.at[i]).start()
-    for fill, copy in zip(fills, copies):
-        fill.wait()
-        copy.start()
-    for i, block in enumerate(blocks):
-        pltpu.make_async_copy(wide.at[block], wg_out.at[block], out_sems.at[i]).wait()
+    for i in range(STORES):
+        block = slice(i * count, (i + 1) * count)
+        for c in range(CHUNKS):
+            wide[i, :, c * part : (c + 1) * part] = wg[c, block].astype(F32) * factor
+        pltpu.make_async_copy(wide.at[i], wg_out.at[block], out_sems.at[i]).start()
+        if i < 3:
+            copies[i].start()
+    for i in range(STORES):
+        block = slice(i * count, (i + 1) * count)
+        pltpu.make_async_copy(wide.at[i], wg_out.at[block], out_sems.at[i]).wait()
     for copy in copies:
         copy.wait()
 
@@ -782,11 +751,11 @@
     outs = pl.pallas_call(
         functools.partial(fused_kernel, nf),
         out_shape=(
-            jax.ShapeDtypeStruct((3, tokens, heads_width), BF16),
-            jax.ShapeDtypeStruct((rows, width), BF16),
+            pltpu.VMEM((3, tokens, heads_width), BF16),
+            pltpu.VMEM((CHUNKS, rows, part), BF16),
         ),
         in_specs=[pl.BlockSpec(memory_space=pltpu.HBM)] * 5,
-        out_specs=[pl.BlockSpec(memory_space=pltpu.HBM)] * 2,
+        out_specs=[pl.BlockSpec(memory_space=pltpu.VMEM)] * 2,
         scratch_shapes=[
             pltpu.VMEM((nf, 2, CHUNKS, tokens, part), BF16),
             pltpu.VMEM((3, nf, 2, tokens, core_rows), BF16),
@@ -804,7 +773,6 @@
             pltpu.VMEM((CHUNKS, half_rows, part), BF16),
             pltpu.VMEM((core_rows, part), BF16),
             pltpu.VMEM((3, half_rows // 2, part), BF16),
-            pltpu.VMEM((CHUNKS, rows, part), BF16),
             dma,
             dma((2, 3, nf)),
             dma((3, nf, 2)),
@@ -829,7 +797,6 @@
             dma((4,)),
             dma((3,)),
             dma((3,)),
-            dma((CHUNKS,)),
         ],
         compiler_params=pltpu.CompilerParams(
             collective_id=0, has_side_effects=True, vmem_limit_bytes=58 * 1024 * 1024
@@ -839,17 +806,14 @@
         functools.partial(store_kernel, 1.0 / samples),
         out_shape=(jax.ShapeDtypeStruct((tokens, heads_width), BF16),) * 3
         + (jax.ShapeDtypeStruct((rows, width), F32),),
-        in_specs=[pl.BlockSpec(memory_space=pltpu.HBM)] * 2,
+        in_specs=[pl.BlockSpec(memory_space=pltpu.VMEM)] * 2,
         out_specs=[pl.BlockSpec(memory_space=pltpu.HBM)] * 4,
         scratch_shapes=[
-            pltpu.VMEM((3, tokens, heads_width), BF16),
-            pltpu.VMEM((rows, width), BF16),
-            pltpu.VMEM((rows, width), F32),
-            dma((2, 3)),
-            dma((STORES,)),
+            pltpu.VMEM((STORES, rows // STORES, width), F32),
+            dma((3,)),
             dma((STORES,)),
         ],
-        compiler_params=pltpu.CompilerParams(vmem_limit_bytes=58 * 1024 * 1024),
+        compiler_params=pltpu.CompilerParams(vmem_limit_bytes=24 * 1024 * 1024),
     )(*outs)
     return tuple(out[None] for out in stored[:3]) + (stored[3],)
 

time: 82.2 us -> 80.7 us (0.982)
  Pallas kernels: 81.2 us -> 79.9 us
    pallas_call x1, Pallas kernels: 3.67 us -> 2.6 us  [fused_body(): pl.pallas_call(functools.partial(store_kernel, 1.0 / samples), out_shape=...]
where the time goes in v3:
time: 80.7 us; the launch traced here: 80.5 us
  Pallas kernels  79.9 us (99%)
    pallas_call x1, Pallas kernels, fused_body(): pl.pallas_call(functools.partial(fused_kernel, nf), out_shape=(pltpu.VMEM...  77.3 us
    pallas_call x1, Pallas kernels, fused_body(): pl.pallas_call(functools.partial(store_kernel, 1.0 / samples), out_shape=...  2.6 us

profile of v3, /device:TPU:1, one launch (start us, length us, event | category | flops | bytes accessed | tf_op | source)
XLA Modules:
  0.0 80.5 jit_solution(7071009162138116960)
XLA Ops:
  0.6 77.3 %shard_map.84 = (bf16[3,128,2048]{2,1,0:T(8,128)(2,1)S(1)}, bf16[4,512,512]{2,1,0:T(8,128)(2,1)S(1)}) custom-call(bf16[128,2048]{1,0:T(8,128)(2,1)} %bitcast.7, bf16[128,2048]{1,0:T(8,128)(2,1)} %bitcast.8, bf16[128,2048]{1,0:T(8,128)(2,1)} %bitcast.9, bf16[128,2048]{1,0:T(8,128)(2,1)} %bitcast.10, bf16[512,2048]{1,0:T(8,128)(2,1)} %w_hbm.1), custom_call_target="tpu_custom_call" | custom-call | tf_op jit(solution)/shard_map/pallas_call | solution.py:751
  77.9 2.6 %shard_map.85 = (bf16[128,2048]{1,0:T(8,128)(2,1)}, bf16[128,2048]{1,0:T(8,128)(2,1)}, bf16[128,2048]{1,0:T(8,128)(2,1)}, f32[512,2048]{1,0:T(8,128)}) custom-call(bf16[3,128,2048]{2,1,0:T(8,128)(2,1)S(1)} %get-tuple-element.10.gr, bf16[4,512,512]{2,1,0:T(8,128)(2,1)S(1)} %get-tuple-element.11.wg), custom_call_target="tpu_custom_call" | custom-call | tf_op jit(solution)/shard_map/pallas_call | solution.py:805

commit v4 on v3

--- a/solution.py
+++ b/solution.py
@@ -597,6 +597,25 @@
         take_other(first, k)
         take_other(third, k)
 
+    def settle(c):
+        for g in range(nf):
+            for which in range(3):
+                far_copy(which, g).wait_send()
+        for j in (first, second, third):
+            at_copy(j).wait_send()
+        for k in range(CHUNKS):
+            own_z(0, k, cot.at[f, core, k]).wait_send()
+            own_z(1, k, cot.at[f, core, k]).wait_send()
+            to_sibling(f, k, cot.at[f, core, k]).wait_send()
+
+        @pl.when(foreign)
+        def _():
+            for g in range(nf):
+                for which in range(3):
+                    near_copy(which, g).wait_send()
+            for k in range(CHUNKS):
+                cross(k).wait_send()
+
     def play(*steps):
         for action, argument in steps:
             action(argument)
@@ -621,22 +640,23 @@
             (weight_term, 3),
             (send_go, third),
             (send_go, first),
+            (reduce_y, 2),
             (reduce_x, 0),
-            (reduce_y, 2),
-            (take_go, first),
             (reduce_x, 1),
-            (gather_y, 0),
             (reduce_direct, last),
             (reduce_x, 2),
+            (settle, 0),
+            (take_go, first),
+            (gather_direct, last),
+            (gather_y, 0),
+            (gather_core, 0),
             (gather_y, 1),
-            (gather_core, 0),
-            (take_go, third),
-            (gather_direct, last),
-            (take_go, second),
-            (gather_y, 2),
             (gather_core, 1),
             (gather_last, last),
+            (gather_y, 2),
             (gather_core, 2),
+            (take_go, second),
+            (take_go, third),
         )
 
     @pl.when(outer)
@@ -652,24 +672,25 @@
             (weight_term, 2),
             (reduce_y, 1),
             (reduce_x, 0),
+            (settle, 0),
             (all_arrive, 3),
             (weight_term, 3),
+            (send_go, first),
+            (send_go, second),
             (send_go, third),
-            (send_go, second),
-            (send_go, first),
             (reduce_y, 2),
             (reduce_x, 1),
-            (gather_y, 0),
             (take_go, second),
             (reduce_direct, last),
+            (reduce_x, 2),
+            (take_go, third),
+            (gather_direct, last),
+            (gather_y, 0),
+            (gather_core, 0),
             (gather_y, 1),
-            (gather_core, 0),
-            (take_go, third),
-            (reduce_x, 2),
-            (gather_direct, last),
             (gather_core, 1),
+            (gather_last, last),
             (gather_y, 2),
-            (gather_last, last),
             (gather_core, 2),
         )
 
@@ -690,15 +711,10 @@
         spread_copy(i).wait_send()
     for j in (first, second, third):
         go_copy(j).wait_send()
-        at_copy(j).wait_send()
     for g in range(nf):
         home_copy(g, 1 - s).wait_send()
-        for which in range(3):
-            far_copy(which, g).wait_send()
     for k in range(CHUNKS):
-        own_z(0, k, cot.at[f, core, k]).wait_send()
-        own_z(1, k, cot.at[f, core, k]).wait_send()
-        for j in range(nf):
+        for j in (first, second, third):
             to_sibling(j, k, cot.at[j, core, k]).wait_send()
 
     @pl.when(inner)
@@ -711,10 +727,6 @@
     def _():
         for g in range(nf):
             home_copy(g, s).wait_send()
-            for which in range(3):
-                near_copy(which, g).wait_send()
-        for k in range(CHUNKS):
-            cross(k).wait_send()
 
 
 def store_kernel(factor, gr, wg, qg_out, kg_out, vg_out, wg_out, wide, sems, out_sems):

time: 80.7 us -> 80.2 us (level)
  no operation moved by 1% of the time
where the time goes in v4:
time: 80.2 us; the launch traced here: 79.9 us
  Pallas kernels  79.3 us (99%)
    pallas_call x1, Pallas kernels, fused_body(): pl.pallas_call(functools.partial(fused_kernel, nf), out_shape=(pltpu.VMEM...  76.7 us
    pallas_call x1, Pallas kernels, fused_body(): pl.pallas_call(functools.partial(store_kernel, 1.0 / samples), out_shape=...  2.6 us

profile of v4, /device:TPU:1, one launch (start us, length us, event | category | flops | bytes accessed | tf_op | source)
XLA Modules:
  0.0 79.9 jit_solution(10998770750199901432)
XLA Ops:
  0.6 76.7 %shard_map.84 = (bf16[3,128,2048]{2,1,0:T(8,128)(2,1)S(1)}, bf16[4,512,512]{2,1,0:T(8,128)(2,1)S(1)}) custom-call(bf16[128,2048]{1,0:T(8,128)(2,1)} %bitcast.7, bf16[128,2048]{1,0:T(8,128)(2,1)} %bitcast.8, bf16[128,2048]{1,0:T(8,128)(2,1)} %bitcast.9, bf16[128,2048]{1,0:T(8,128)(2,1)} %bitcast.10, bf16[512,2048]{1,0:T(8,128)(2,1)} %w_hbm.1), custom_call_target="tpu_custom_call" | custom-call | tf_op jit(solution)/shard_map/pallas_call | solution.py:763
  77.4 2.6 %shard_map.85 = (bf16[128,2048]{1,0:T(8,128)(2,1)}, bf16[128,2048]{1,0:T(8,128)(2,1)}, bf16[128,2048]{1,0:T(8,128)(2,1)}, f32[512,2048]{1,0:T(8,128)}) custom-call(bf16[3,128,2048]{2,1,0:T(8,128)(2,1)S(1)} %get-tuple-element.10.gr, bf16[4,512,512]{2,1,0:T(8,128)(2,1)S(1)} %get-tuple-element.11.wg), custom_call_target="tpu_custom_call" | custom-call | tf_op jit(solution)/shard_map/pallas_call | solution.py:817

commit v5 on v4

--- a/solution.py
+++ b/solution.py
@@ -9,7 +9,8 @@
 
 DH = 128
 LOG2E = 1.4426950408889634
-CHUNKS = 4
+SHARES = (5, 4, 4, 3)
+CHUNKS = len(SHARES)
 STORES = 8
 F32 = jnp.float32
 BF16 = jnp.bfloat16
@@ -126,6 +127,12 @@
 
 def dot_tn(a, b):
     return lax.dot_general(a, b, (((0,), (0,)), ((), ())), preferred_element_type=F32)
+
+
+def chunk_widths(width):
+    unit = width // sum(SHARES)
+    widths = [share * unit for share in SHARES]
+    return widths, [sum(widths[:k]) for k in range(CHUNKS)]
 
 
 def fused_kernel(
@@ -180,7 +187,7 @@
 ):
     tokens, width = c_hbm.shape
     rows = w_hbm.shape[0]
-    part = width // CHUNKS
+    widths, starts = chunk_widths(width)
     core_rows = rows // 2
     half_rows = core_rows // 2
     group_heads = core_rows // DH
@@ -222,8 +229,11 @@
     def head_cols(g, c):
         return pl.ds(pl.multiple_of(g * rows + c * core_rows, core_rows), core_rows)
 
+    def chunk_cols(k):
+        return slice(starts[k], starts[k] + widths[k])
+
     def chunk(k):
-        return c_hbm.at[:, k * part : (k + 1) * part]
+        return c_hbm.at[:, starts[k] : starts[k] + widths[k]]
 
     def group_at(i):
         return (f + 1 + i) % nf
@@ -255,23 +265,23 @@
         )
 
     def own_local(k):
-        return pltpu.make_async_copy(chunk(k), cot.at[f, core, k], cot_recv.at[f, core, k])
+        return pltpu.make_async_copy(chunk(k), cot[k].at[f, core], cot_recv.at[f, core, k])
 
     def own_z(lane, k, src):
         return remote(
             src,
-            cot.at[f, core, k],
+            cot[k].at[f, core],
             cot_z.at[lane, k],
             cot_recv.at[f, core, k],
             {"fsdp": (first, second)[lane]},
         )
 
     def to_sibling(j, k, src):
-        return remote(src, cot.at[j, core, k], cot_sib.at[j, k], cot_recv.at[j, core, k], sibling)
+        return remote(src, cot[k].at[j, core], cot_sib.at[j, k], cot_recv.at[j, core, k], sibling)
 
     def cross(k):
         return remote(
-            chunk(k), cot.at[f, 1 - core, k], cot_x.at[k], cot_recv.at[f, 1 - core, k], diagonal
+            chunk(k), cot[k].at[f, 1 - core], cot_x.at[k], cot_recv.at[f, 1 - core, k], diagonal
         )
 
     def passed(i):
@@ -279,7 +289,7 @@
 
     def pass_on(i, k):
         j = passed(i)
-        block = cot.at[j, core, k]
+        block = cot[k].at[j, core]
         return remote(block, block, cot_fw.at[i, k], cot_recv.at[j, core, k], {"fsdp": end})
 
     def go_copy(j):
@@ -399,20 +409,20 @@
         total = None
         for k in range(CHUNKS):
             term = dot_nt(
-                cot[j, :, k].reshape(length, part), w_ref[:, k * part : (k + 1) * part]
+                cot[k][j].reshape(length, widths[k]), w_ref[:, starts[k] : starts[k] + widths[k]]
             )
             total = term if total is None else total + term
         return total.astype(BF16)
 
     def take(j, k):
-        wait_into(cot.at[j, core, k], cot_recv.at[j, core, k])
+        wait_into(cot[k].at[j, core], cot_recv.at[j, core, k])
 
     def take_other(j, k):
-        wait_into(cot.at[j, 1 - core, k], cot_recv.at[j, 1 - core, k])
+        wait_into(cot[k].at[j, 1 - core], cot_recv.at[j, 1 - core, k])
 
     def share(j, k):
         take(j, k)
-        to_sibling(j, k, cot.at[j, core, k]).start()
+        to_sibling(j, k, cot[k].at[j, core]).start()
 
     def urgent(k):
         @pl.when(inner)
@@ -421,13 +431,13 @@
                 j = passed(i)
                 take(j, k)
                 pass_on(i, k).start()
-                to_sibling(j, k, cot.at[j, core, k]).start()
+                to_sibling(j, k, cot[k].at[j, core]).start()
 
     def pass_own(k):
         take(f, k)
-        own_z(0, k, cot.at[f, core, k]).start()
-        own_z(1, k, cot.at[f, core, k]).start()
-        to_sibling(f, k, cot.at[f, core, k]).start()
+        own_z(0, k, cot[k].at[f, core]).start()
+        own_z(1, k, cot[k].at[f, core]).start()
+        to_sibling(f, k, cot[k].at[f, core]).start()
 
     def for_native(*chunks):
         @pl.when(native)
@@ -480,12 +490,12 @@
     def reduce_copy(stage, c):
         src, dst = ((y_out, y_in), (x_out, x_in))[stage]
         device = (across, partner)[stage]
-        return remote(src.at[c], dst.at[c], rs_send.at[stage, c], rs_recv.at[stage, c], device)
+        return remote(src[c], dst[c], rs_send.at[stage, c], rs_recv.at[stage, c], device)
 
     def gather_copy(stage, c):
         which = half if stage < 2 else 1 - half
         base = core * core_rows + which * half_rows
-        block = final.at[c, pl.ds(pl.multiple_of(base, half_rows), half_rows)]
+        block = final.at[pl.ds(pl.multiple_of(base, half_rows), half_rows), chunk_cols(c)]
         device = (across, sibling, sibling)[stage]
         return remote(block, block, ag_send.at[stage, c], ag_recv.at[stage, c], device)
 
@@ -503,7 +513,7 @@
 
     def piece(c, h, t):
         base = core * core_rows + (h * 2 + t) * (half_rows // 2)
-        return final.at[last, pl.ds(pl.multiple_of(base, half_rows // 2), half_rows // 2)]
+        return final.at[pl.ds(pl.multiple_of(base, half_rows // 2), half_rows // 2), chunk_cols(last)]
 
     def spread_copy(i):
         block = piece(core, half, s)
@@ -520,17 +530,17 @@
             for d in (first, second, third):
                 wait_into(at_in.at[d], at_recv.at[d])
         at_all = at_in[...].reshape(nf * length, core_rows)
-        acc[c] = dot_tn(at_all, cot[:, :, c].reshape(nf * length, part))
+        acc[c][...] = dot_tn(at_all, cot[c][...].reshape(nf * length, widths[c]))
         if c < last:
-            y_out[c] = acc[c, theirs()].astype(BF16)
+            y_out[c][...] = acc[c][theirs()].astype(BF16)
             reduce_copy(0, c).start()
         else:
-            d_out[...] = acc[c].astype(BF16)
+            d_out[...] = acc[c][...].astype(BF16)
             for i in (2, 1, 0):
                 direct_copy(i).start()
 
     def reduce_direct(c):
-        total = acc[last, quarter_of(half, s)]
+        total = acc[last][quarter_of(half, s)]
         for i in range(3):
             direct_copy(i).wait_recv()
             total = total + d_in[i].astype(F32)
@@ -550,14 +560,14 @@
 
     def reduce_y(c):
         reduce_copy(0, c).wait_recv()
-        x_out[c] = (acc[c, mine()] + y_in[c].astype(F32)).astype(BF16)
+        x_out[c][...] = (acc[c][mine()] + y_in[c][...].astype(F32)).astype(BF16)
         reduce_copy(1, c).start()
 
     def reduce_x(c):
         reduce_copy(1, c).wait_recv()
         base = core * core_rows + half * half_rows
-        final[c, pl.ds(pl.multiple_of(base, half_rows), half_rows)] = (
-            x_out[c].astype(F32) + x_in[c].astype(F32)
+        final[pl.ds(pl.multiple_of(base, half_rows), half_rows), chunk_cols(c)] = (
+            x_out[c][...].astype(F32) + x_in[c][...].astype(F32)
         ).astype(BF16)
         gather_copy(0, c).start()
         gather_copy(1, c).start()
@@ -604,9 +614,9 @@
         for j in (first, second, third):
             at_copy(j).wait_send()
         for k in range(CHUNKS):
-            own_z(0, k, cot.at[f, core, k]).wait_send()
-            own_z(1, k, cot.at[f, core, k]).wait_send()
-            to_sibling(f, k, cot.at[f, core, k]).wait_send()
+            own_z(0, k, cot[k].at[f, core]).wait_send()
+            own_z(1, k, cot[k].at[f, core]).wait_send()
+            to_sibling(f, k, cot[k].at[f, core]).wait_send()
 
         @pl.when(foreign)
         def _():
@@ -715,7 +725,7 @@
         home_copy(g, 1 - s).wait_send()
     for k in range(CHUNKS):
         for j in (first, second, third):
-            to_sibling(j, k, cot.at[j, core, k]).wait_send()
+            to_sibling(j, k, cot[k].at[j, core]).wait_send()
 
     @pl.when(inner)
     def _():
@@ -730,16 +740,14 @@
 
 
 def store_kernel(factor, gr, wg, qg_out, kg_out, vg_out, wg_out, wide, sems, out_sems):
-    count = wg.shape[1] // STORES
-    part = wg.shape[2]
+    count = wg.shape[0] // STORES
     copies = [
         pltpu.make_async_copy(gr.at[i], dst, sems.at[i])
         for i, dst in enumerate((qg_out, kg_out, vg_out))
     ]
     for i in range(STORES):
         block = slice(i * count, (i + 1) * count)
-        for c in range(CHUNKS):
-            wide[i, :, c * part : (c + 1) * part] = wg[c, block].astype(F32) * factor
+        wide[i] = wg[block].astype(F32) * factor
         pltpu.make_async_copy(wide.at[i], wg_out.at[block], out_sems.at[i]).start()
         if i < 3:
             copies[i].start()
@@ -754,7 +762,7 @@
     samples = lax.axis_size("dp") * nf
     tokens, heads_width = queries.shape[1:]
     rows, width = out_weight.shape
-    part = width // CHUNKS
+    widths = chunk_widths(width)[0]
     core_rows = rows // 2
     half_rows = core_rows // 2
     length = 2 * tokens
@@ -764,12 +772,12 @@
         functools.partial(fused_kernel, nf),
         out_shape=(
             pltpu.VMEM((3, tokens, heads_width), BF16),
-            pltpu.VMEM((CHUNKS, rows, part), BF16),
+            pltpu.VMEM((rows, width), BF16),
         ),
         in_specs=[pl.BlockSpec(memory_space=pltpu.HBM)] * 5,
         out_specs=[pl.BlockSpec(memory_space=pltpu.VMEM)] * 2,
         scratch_shapes=[
-            pltpu.VMEM((nf, 2, CHUNKS, tokens, part), BF16),
+            tuple(pltpu.VMEM((nf, 2, tokens, part), BF16) for part in widths),
             pltpu.VMEM((3, nf, 2, tokens, core_rows), BF16),
             pltpu.VMEM((nf, length, core_rows), BF16),
             pltpu.VMEM((nf, length, core_rows), BF16),
@@ -778,13 +786,13 @@
             pltpu.VMEM((heads, length, length), F32),
             pltpu.VMEM((nf, 2, 3, tokens, core_rows), BF16),
             pltpu.VMEM((core_rows, width), BF16),
-            pltpu.VMEM((CHUNKS, core_rows, part), F32),
-            pltpu.VMEM((CHUNKS, half_rows, part), BF16),
-            pltpu.VMEM((CHUNKS, half_rows, part), BF16),
-            pltpu.VMEM((CHUNKS, half_rows, part), BF16),
-            pltpu.VMEM((CHUNKS, half_rows, part), BF16),
-            pltpu.VMEM((core_rows, part), BF16),
-            pltpu.VMEM((3, half_rows // 2, part), BF16),
+            tuple(pltpu.VMEM((core_rows, part), F32) for part in widths),
+            tuple(pltpu.VMEM((half_rows, part), BF16) for part in widths),
+            tuple(pltpu.VMEM((half_rows, part), BF16) for part in widths),
+            tuple(pltpu.VMEM((half_rows, part), BF16) for part in widths),
+            tuple(pltpu.VMEM((half_rows, part), BF16) for part in widths),
+            pltpu.VMEM((core_rows, widths[-1]), BF16),
+            pltpu.VMEM((3, half_rows // 2, widths[-1]), BF16),
             dma,
             dma((2, 3, nf)),
             dma((3, nf, 2)),

time: 80.2 us -> 79.9 us (level)
  no operation moved by 1% of the time
where the time goes in v5:
time: 79.9 us; the launch traced here: 79.8 us
  Pallas kernels  78.9 us (99%)
  between operations  0.82 us (1%)
    pallas_call x1, Pallas kernels, fused_body(): pl.pallas_call(functools.partial(fused_kernel, nf), out_shape=(pltpu.VMEM...  76.3 us
    pallas_call x1, Pallas kernels, fused_body(): pl.pallas_call(functools.partial(store_kernel, 1.0 / samples), out_shape=...  2.6 us

profile of v5, /device:TPU:1, one launch (start us, length us, event | category | flops | bytes accessed | tf_op | source)
XLA Modules:
  0.0 79.8 jit_solution(12290724663916113361)
XLA Ops:
  0.6 76.3 %shard_map.84 = (bf16[3,128,2048]{2,1,0:T(8,128)(2,1)S(1)}, bf16[512,2048]{1,0:T(8,128)(2,1)S(1)}) custom-call(bf16[128,2048]{1,0:T(8,128)(2,1)} %bitcast.7, bf16[128,2048]{1,0:T(8,128)(2,1)} %bitcast.8, bf16[128,2048]{1,0:T(8,128)(2,1)} %bitcast.9, bf16[128,2048]{1,0:T(8,128)(2,1)} %bitcast.10, bf16[512,2048]{1,0:T(8,128)(2,1)} %w_hbm.1), custom_call_target="tpu_custom_call" | custom-call | tf_op jit(solution)/shard_map/pallas_call | solution.py:771
  77.0 2.6 %shard_map.85 = (bf16[128,2048]{1,0:T(8,128)(2,1)}, bf16[128,2048]{1,0:T(8,128)(2,1)}, bf16[128,2048]{1,0:T(8,128)(2,1)}, f32[512,2048]{1,0:T(8,128)}) custom-call(bf16[3,128,2048]{2,1,0:T(8,128)(2,1)S(1)} %get-tuple-element.10.gr, bf16[512,2048]{1,0:T(8,128)(2,1)S(1)} %get-tuple-element.11.wg), custom_call_target="tpu_custom_call" | custom-call | tf_op jit(solution)/shard_map/pallas_call | solution.py:825

commit v6 on v5

--- a/solution.py
+++ b/solution.py
@@ -654,9 +654,9 @@
             (reduce_x, 0),
             (reduce_x, 1),
             (reduce_direct, last),
-            (reduce_x, 2),
             (settle, 0),
             (take_go, first),
+            (reduce_x, 2),
             (gather_direct, last),
             (gather_y, 0),
             (gather_core, 0),

time: 79.9 us -> 79.9 us (level)
  no operation moved by 1% of the time
where the time goes in v6:
time: 79.9 us; the launch traced here: 79.8 us
  Pallas kernels  78.9 us (99%)
  between operations  0.82 us (1%)
    pallas_call x1, Pallas kernels, fused_body(): pl.pallas_call(functools.partial(fused_kernel, nf), out_shape=(pltpu.VMEM...  76.3 us
    pallas_call x1, Pallas kernels, fused_body(): pl.pallas_call(functools.partial(store_kernel, 1.0 / samples), out_shape=...  2.6 us

profile of v6, /device:TPU:1, one launch (start us, length us, event | category | flops | bytes accessed | tf_op | source)
XLA Modules:
  0.0 79.8 jit_solution(15611273730625106623)
XLA Ops:
  0.6 76.3 %shard_map.84 = (bf16[3,128,2048]{2,1,0:T(8,128)(2,1)S(1)}, bf16[512,2048]{1,0:T(8,128)(2,1)S(1)}) custom-call(bf16[128,2048]{1,0:T(8,128)(2,1)} %bitcast.7, bf16[128,2048]{1,0:T(8,128)(2,1)} %bitcast.8, bf16[128,2048]{1,0:T(8,128)(2,1)} %bitcast.9, bf16[128,2048]{1,0:T(8,128)(2,1)} %bitcast.10, bf16[512,2048]{1,0:T(8,128)(2,1)} %w_hbm.1), custom_call_target="tpu_custom_call" | custom-call | tf_op jit(solution)/shard_map/pallas_call | solution.py:771
  77.0 2.6 %shard_map.85 = (bf16[128,2048]{1,0:T(8,128)(2,1)}, bf16[128,2048]{1,0:T(8,128)(2,1)}, bf16[128,2048]{1,0:T(8,128)(2,1)}, f32[512,2048]{1,0:T(8,128)}) custom-call(bf16[3,128,2048]{2,1,0:T(8,128)(2,1)S(1)} %get-tuple-element.10.gr, bf16[512,2048]{1,0:T(8,128)(2,1)S(1)} %get-tuple-element.11.wg), custom_call_target="tpu_custom_call" | custom-call | tf_op jit(solution)/shard_map/pallas_call | solution.py:825
